TPU v7x, 256 devices: a whole 4x4x8 slice. The times are simulated.
256 devices in a mesh: store: 64 (over z, x, core), batch: 4 (over y).
Axes of the slice: x: 4, y: 4, z: 8, core: 2. Of those that a mesh axis runs over, the one named last changes fastest.
Arguments:
- queries: bfloat16 [32768, 1152], P(('store', 'batch')), may hold values from -6 to 6
- query_cluster: int32 [32768], P(('store', 'batch')), may hold values from 0 to 63, as said below
- store: bfloat16 [131072, 1152], P('store'), may hold values from -6 to 6
- store_counts: int32 [64], replicated, may hold values from 2 to 2048, as said below
Outputs:
- best_two: float32 [32768, 2], P(('store', 'batch'))
- novelty: float32 [32768], P(('store', 'batch'))
- neighbours: float32 [32768, 1152], P(('store', 'batch'))
Inputs may be any that keep to these rules, and one draw needn't show every extreme that they name: `query_cluster`: among the rows of one device every cluster appears at least once and none more than 4 times; on every device of one batch index one cluster, drawn for that index, appears exactly 4 times. `store_counts`: at least one cluster has all 2048 rows live.
All inputs are finite; a program needn't handle non-finite values.
Results may differ from a plain program's by a relative error of at most 0.0008.
Values may be sent and summed in bfloat16 or wider, within the bound.
No kernel may reach another device: no remote copies, remote signals or barrier semaphores. Data moves between devices by JAX's collectives and lax.ppermute only.
A program may use at most 64 MiB of HBM per device.

v0:
```python
import math

import jax
import jax.numpy as jnp
from jax import lax
from jax.sharding import PartitionSpec as P

normalized_sharpness = 160.0
epsilon = 1e-06


def inverse_norms(block_of):
    wide = block_of.astype(jnp.float32)
    return lax.rsqrt(jnp.sum(wide * wide, axis=1) + epsilon)


def leading_pair(values):
    first = jnp.max(values, axis=1)
    equal_count = jnp.sum((values == first[:, None]).astype(jnp.int32), axis=1)
    below = jnp.max(jnp.where(values < first[:, None], values, -3.0), axis=1)
    second = jnp.where(equal_count >= 2, first, below)
    return jnp.stack([first, second], axis=1)


def cosines(queries_in, queries_scale, block_of, scale_part, active_indicator):
    raw_dot = lax.dot_general(
        queries_in, block_of, (((1,), (1,)), ((), ())), preferred_element_type=jnp.float32
    )
    return jnp.where(
        active_indicator[None, :], raw_dot * queries_scale[:, None] * scale_part[None, :], -2.0
    )


def cosine_rows(queries_in, block_rows, scale_rows, live_count):
    queries_scale = inverse_norms(queries_in)
    row_span = block_rows.shape[0]
    active_indicator = lax.iota(jnp.int32, row_span) < live_count
    return cosines(queries_in, queries_scale, block_rows, scale_rows, active_indicator)


def weigh_rows(angular_similarity, block_rows, live_count, maximum_entry):
    row_span = block_rows.shape[0]
    active_indicator = lax.iota(jnp.int32, row_span) < live_count
    exponential_summands = jnp.where(
        active_indicator[None, :],
        jnp.exp(normalized_sharpness * (angular_similarity - maximum_entry)),
        0.0,
    )
    return (
        jnp.sum(exponential_summands, axis=1),
        jnp.dot(
            exponential_summands.astype(jnp.bfloat16),
            block_rows,
            preferred_element_type=jnp.float32,
        ),
    )


def body(queries, query_cluster, store, store_counts):
    n_store = lax.axis_size("store")
    n_batch = lax.axis_size("batch")
    rows_dev, features = queries.shape
    clusters = store_counts.shape[0]
    slot_depth = 2 * rows_dev // clusters
    total_rows = rows_dev * n_store * n_batch
    growth = math.log(3.0) / total_rows
    labels = lax.iota(jnp.int32, clusters)
    member = query_cluster[:, None] == labels[None, :]
    member_int = member.astype(jnp.int32)
    rank_in = jnp.sum((jnp.cumsum(member_int, axis=0) - member_int) * member_int, axis=1)
    slot_of = query_cluster * slot_depth + rank_in
    local_index = lax.iota(jnp.int32, rows_dev)
    send_rows = jnp.zeros((clusters * slot_depth, features), jnp.bfloat16).at[slot_of].set(queries)
    send_rows = send_rows.reshape(clusters, slot_depth, features)
    send_pos = jnp.full((clusters * slot_depth,), -1, jnp.int32).at[slot_of].set(local_index)
    send_pos = send_pos.reshape(clusters, slot_depth)
    live_count = store_counts[lax.axis_index("store")]
    store_scale = inverse_norms(store)
    got_rows = lax.all_to_all(send_rows, "store", split_axis=0, concat_axis=0, tiled=True)
    got_pos = lax.all_to_all(send_pos, "store", split_axis=0, concat_axis=0, tiled=True)
    sources, item_count = got_pos.shape
    flattened = got_rows.reshape(sources * item_count, features)
    angular_similarity = cosine_rows(flattened, store, store_scale, live_count)
    foremost_couple = leading_pair(angular_similarity)
    exp_total, weighted = weigh_rows(angular_similarity, store, live_count, foremost_couple[:, :1])
    result = weighted / exp_total[:, None]
    near_slots = result.reshape(sources, item_count, features)
    best_slots = foremost_couple.reshape(sources, item_count, 2)
    back_near, back_best = (
        lax.all_to_all(near_slots, "store", split_axis=0, concat_axis=0, tiled=True),
        lax.all_to_all(best_slots, "store", split_axis=0, concat_axis=0, tiled=True),
    )
    neighbours = back_near.reshape(clusters * slot_depth, features)[slot_of]
    best_two = back_best.reshape(clusters * slot_depth, 2)[slot_of]
    own_index = (
        lax.axis_index("store") * n_batch + lax.axis_index("batch")
    ) * rows_dev + local_index
    recency = jnp.exp(own_index.astype(jnp.float32) * growth)
    belonging_real = member.astype(jnp.float32)
    top_cos = best_two[:, 0]
    totals = lax.psum(
        (
            jnp.sum(belonging_real * (recency * top_cos)[:, None], axis=0),
            jnp.sum(belonging_real * recency[:, None], axis=0),
        ),
        ("store", "batch"),
    )
    cluster_ratio = totals[0] / totals[1]
    novelty = top_cos - jnp.sum(belonging_real * cluster_ratio[None, :], axis=1)
    return (best_two, novelty, neighbours)


def solution(mesh):
    in_specs = (P(("store", "batch"), None), P(("store", "batch")), P("store", None), P())
    out_specs = (P(("store", "batch"), None), P(("store", "batch")), P(("store", "batch"), None))
    return jax.shard_map(body, mesh=mesh, in_specs=in_specs, out_specs=out_specs, check_vma=False)
```

profile of v0, /device:TPU:1, one launch (start us, length us, event | category | flops | bytes accessed | tf_op | source)
XLA Modules:
  0.0 149.2 jit_solution(2964758644651478213)
XLA Ops:
  0.6 0.7 fusion.12
  1.4 0.2 reduce_window_sum.11
  1.6 0.8 select_reduce_fusion.3
  2.4 0.7 compare_select_fusion.1
  3.1 1.8 %scatter_custom_fusion = bf16[256,1152]{1,0:T(8,128)(2,1)S(1)} fusion(s32[128]{0:T(128)S(1)} %compare_select_fusion.1, bf16[128,1152]{1,0:T(8,128)(2,1)} %param.4, bf16[]{:T(256)} %constant.9.clone.1), kind=kCustom, calls=%fused_computation.19 | custom fusion | bytes 590336 | tf_op jit(solution)/shard_map/scatter | solution.py:73
  4.8 1.0 reshape.98
  5.8 13.0 %all-to-all-start = ((bf16[64,4,1152]{2,1,0:T(4,128)(2,1)}), bf16[64,4,1152]{2,1,0:T(4,128)(2,1)S(1)}, u32[]{:S(2)}, u32[]{:S(2)}) async-start(bf16[64,4,1152]{2,1,0:T(4,128)(2,1)} %reshape.98), calls=%async_computation | async-start | bytes 1179648 | tf_op jit(solution)/shard_map/all_to_all | solution.py:79
  18.8 0.6 dynamic_slice.3
  19.4 0.7 iota_compare_fusion.1
  20.0 3.3 %multiply_reduce_fusion = f32[2048]{0:T(1024)S(1)} fusion(bf16[2048,1152]{1,0:T(8,128)(2,1)} %param.6), kind=kLoop, calls=%fused_computation.3 | loop fusion | flops 7075840 | bytes 4726784 | tf_op jit(solution)/shard_map/reduce_sum | solution.py:14
  23.4 14.4 %all-to-all-done = bf16[64,4,1152]{2,1,0:T(4,128)(2,1)S(1)} async-done(((bf16[64,4,1152]{2,1,0:T(4,128)(2,1)}), bf16[64,4,1152]{2,1,0:T(4,128)(2,1)S(1)}, u32[]{:S(2)}, u32[]{:S(2)}) %all-to-all-start) | async-done | bytes 589856 | tf_op jit(solution)/shard_map/all_to_all | solution.py:79
  37.8 0.4 multiply_reduce_fusion.1
  38.3 0.1 reshape.99
  38.5 4.0 %fusion.15 = (f32[256]{0:T(256)S(1)}, f32[256,2048]{1,0:T(8,128)S(1)}) fusion(f32[2048]{0:T(1024)S(1)} %add_rsqrt_fusion.1, f32[256]{0:T(256)S(1)} %rsqrt.18, bf16[256,1152]{1,0:T(8,128)(2,1)S(1)} %reshape.99, bf16[2048,1152]{1,0:T(8,128)(2,1)} %param.6, pred[2048]{0:T(1024)(128)(4,1)S(1)} %iota_compare_fusion.1), kind=kOutput, calls=%fused_computation.39 | convolution fusion | flops 1210056448 | bytes 7417856 | tf_op jit(solution)/shard_map/dot_general | solution.py:26
  42.5 0.1 stack.7
  42.6 0.4 convert_reduce_fusion
  43.0 0.8 fusion.3
  43.7 0.1 ge.19
  44.0 0.7 copy.18
  44.7 5.8 %all-to-all-start.1 = ((f32[64,4,2]{1,2,0:T(2,128)}), f32[64,4,2]{1,2,0:T(2,128)S(1)}, u32[]{:S(2)}, u32[]{:S(2)}) async-start(f32[64,4,2]{1,2,0:T(2,128)} %copy.18), calls=%async_computation.1 | async-start | bytes 131072 | tf_op jit(solution)/shard_map/all_to_all | solution.py:91
  50.5 3.9 %convolution_divide_fusion = f32[256,1152]{1,0:T(8,128)S(1)} fusion(bf16[2048,1152]{1,0:T(8,128)(2,1)} %param.6, f32[256,2048]{1,0:T(8,128)S(1)} %get-tuple-element.25, f32[256]{0:T(256)S(1)} %get-tuple-element.24, pred[2048]{0:T(1024)(128)(4,1)S(1)} %iota_compare_fusion.1, f32[256]{0:T(256)S(1)} %get-tuple-element.18), kind=kOutput, calls=%fused_computation.7 | convolution fusion | flops 1210351616 | bytes 7999488 | tf_op jit(solution)/shard_map/dot_general | solution.py:51
  54.4 1.4 reshape.101
  55.7 4.8 %all-to-all-done.1 = f32[64,4,2]{1,2,0:T(2,128)S(1)} async-done(((f32[64,4,2]{1,2,0:T(2,128)}), f32[64,4,2]{1,2,0:T(2,128)S(1)}, u32[]{:S(2)}, u32[]{:S(2)}) %all-to-all-start.1) | async-done | bytes 2080 | tf_op jit(solution)/shard_map/all_to_all | solution.py:91
  60.6 5.6 %all-to-all-start.2 = ((f32[64,4,1152]{2,1,0:T(4,128)}), f32[64,4,1152]{2,1,0:T(4,128)S(1)}, u32[]{:S(2)}, u32[]{:S(2)}) async-start(f32[64,4,1152]{2,1,0:T(4,128)} %reshape.101), calls=%async_computation.2 | async-start | bytes 2359296 | tf_op jit(solution)/shard_map/all_to_all | solution.py:90
  66.2 0.5 copy.19
  66.7 0.6 gather_fusion
  67.5 0.1 select_reduce_fusion.1
  67.6 78.8 %all-reduce = (f32[64]{0:T(128)S(1)}, f32[64]{0:T(128)S(1)}) all-reduce(f32[64]{0:T(128)S(1)} %get-tuple-element.21, f32[64]{0:T(128)S(1)} %get-tuple-element.20), channel_id=1, replica_groups=mesh['store'=64,'batch'=4] {'store','batch'}, use_global_device_ids=true, to_apply=%region_9.10 | all-reduce | flops 128 | bytes 1024 | tf_op jit(solution)/shard_map/psum | solution.py:101
  146.4 0.2 select_reduce_fusion
  146.6 0.5 bitcast_subtract_fusion
  147.2 0.4 reshape.102
  147.6 1.7 %gather_fusion.1 = f32[128,1152]{1,0:T(8,128)} fusion(f32[256,1152]{1,0:T(8,128)S(1)} %reshape.102, s32[1024]{0:T(1024)S(1)} %pad_clamp_fusion), kind=kCustom, calls=%fused_computation.1 | custom fusion | bytes 1180160 | tf_op jit(solution)/shard_map/gather | solution.py:93
  (19 shorter events, 0.4 us)
Async XLA Ops:
  0.6 18.2 %copy-start.2 = (s32[64]{0:T(128)S(1)}, s32[64]{0:T(128)}, u32[]{:S(2)}) copy-start(s32[64]{0:T(128)} %param.7) | copy-start | bytes 772
  5.8 32.0 %all-to-all-start = ((bf16[64,4,1152]{2,1,0:T(4,128)(2,1)}), bf16[64,4,1152]{2,1,0:T(4,128)(2,1)S(1)}, u32[]{:S(2)}, u32[]{:S(2)}) async-start(bf16[64,4,1152]{2,1,0:T(4,128)(2,1)} %reshape.98), calls=%async_computation | async-start | bytes 1179648 | tf_op jit(solution)/shard_map/all_to_all | solution.py:79
  44.7 15.9 %all-to-all-start.1 = ((f32[64,4,2]{1,2,0:T(2,128)}), f32[64,4,2]{1,2,0:T(2,128)S(1)}, u32[]{:S(2)}, u32[]{:S(2)}) async-start(f32[64,4,2]{1,2,0:T(2,128)} %copy.18), calls=%async_computation.1 | async-start | bytes 131072 | tf_op jit(solution)/shard_map/all_to_all | solution.py:91
  55.7 11.7 %copy-start = (s32[128]{0:T(128)S(1)}, s32[128]{0:T(128)}, u32[]{:S(2)}) copy-start(s32[128]{0:T(128)} %param.5) | copy-start | bytes 1540
  60.6 86.6 %all-to-all-start.2 = ((f32[64,4,1152]{2,1,0:T(4,128)}), f32[64,4,1152]{2,1,0:T(4,128)S(1)}, u32[]{:S(2)}, u32[]{:S(2)}) async-start(f32[64,4,1152]{2,1,0:T(4,128)} %reshape.101), calls=%async_computation.2 | async-start | bytes 2359296 | tf_op jit(solution)/shard_map/all_to_all | solution.py:90
  67.4 81.8 %copy-start.1 = (f32[128,2]{0,1:T(2,128)}, f32[128,2]{0,1:T(2,128)S(1)}, u32[]{:S(2)}) copy-start(f32[128,2]{0,1:T(2,128)S(1)} %copy.21) | copy-start | bytes 3076
where the time goes:
time: 150 us; the launch traced here: 149 us
  blocking collectives  78.8 us (53%)
  starting transfers between devices  24.4 us (16%)
  waiting for transfers between devices  19.3 us (13%)
  local copies, waits for them, and re-layouts  9.2 us (6%)
  other arithmetic  8.81 us (6%)
  matrix products  7.93 us (5%)
    psum x1, blocking collectives, body(): lax.psum((jnp.sum(belonging_real * (recency * top_cos)[:, None], axis=0),...  78.8 us
    all_to_all x1, waiting for transfers between devices, body(): lax.all_to_all(send_rows, 'store', split_axis=0, concat_axis=0, tiled=True)  14.4 us
    all_to_all x1, starting transfers between devices, body(): lax.all_to_all(send_rows, 'store', split_axis=0, concat_axis=0, tiled=True)  13 us
    all_to_all x1, starting transfers between devices, body(): lax.all_to_all(best_slots, 'store', split_axis=0, concat_axis=0, tiled=True)  5.78 us
    all_to_all x1, starting transfers between devices, body(): lax.all_to_all(near_slots, 'store', split_axis=0, concat_axis=0, tiled=True)  5.62 us
    all_to_all x1, waiting for transfers between devices, body(): lax.all_to_all(best_slots, 'store', split_axis=0, concat_axis=0, tiled=True)  4.81 us
    dot_general x1, matrix products, cosines(): lax.dot_general(queries_in, block_of, (((1,), (1,)), ((), ())), preferred...  4 us
    dot_general x1, matrix products, weigh_rows(): jnp.dot(exponential_summands.astype(jnp.bfloat16), block_rows, preferred_...  3.92 us
  transfers between devices with their start and end apart: 3, of which 2 were waited for; matrix products, arithmetic and copies ran while one was open for 8% of the time, Pallas kernels for 0%

commit v1 on v0

v1 whole, which is shorter than its diff:
```python
import math

import jax
import jax.numpy as jnp
from jax import lax
from jax.sharding import PartitionSpec as P

normalized_sharpness = 160.0
epsilon = 1e-06
EXTRA = 128
ROW_SCALE = 8192.0
LOW_SCALE = 4096.0


def inverse_norms(block_of):
    wide = block_of.astype(jnp.float32)
    return lax.rsqrt(jnp.sum(wide * wide, axis=1) + epsilon)


def leading_pair(values):
    first = jnp.max(values, axis=1)
    equal_count = jnp.sum((values == first[:, None]).astype(jnp.int32), axis=1)
    below = jnp.max(jnp.where(values < first[:, None], values, -3.0), axis=1)
    second = jnp.where(equal_count >= 2, first, below)
    return first, second


def split_parts(value):
    high = lax.reduce_precision(value, 5, 10)
    low = (value - high) * LOW_SCALE
    return high.astype(jnp.float16), low.astype(jnp.float16)


def over_batch(value):
    n = lax.axis_size("batch")
    total = value
    for k in range(1, n):
        total = total + lax.ppermute(value, "batch", [(i, (i + k) % n) for i in range(n)])
    return total


def body(queries, query_cluster, store, store_counts):
    n_store = lax.axis_size("store")
    n_batch = lax.axis_size("batch")
    rows_dev, features = queries.shape
    clusters = store_counts.shape[0]
    crows = store.shape[0]
    slot_depth = 2 * rows_dev // clusters
    slots = clusters * slot_depth
    total_rows = rows_dev * n_store * n_batch
    growth = math.log(3.0) / total_rows

    local_index = lax.iota(jnp.int32, rows_dev)
    earlier = (query_cluster[:, None] == query_cluster[None, :]) & (
        local_index[None, :] < local_index[:, None]
    )
    rank_in = jnp.sum(earlier.astype(jnp.int32), axis=1)
    slot_of = query_cluster * slot_depth + rank_in

    lane = lax.iota(jnp.int32, EXTRA)
    tail = jnp.where(
        lane[None, :] == 0,
        local_index.astype(jnp.bfloat16)[:, None],
        jnp.where(lane[None, :] == 1, 1.0, 0.0).astype(jnp.bfloat16),
    )
    wide_rows = jnp.concatenate([queries, tail], axis=1)
    place = (lax.iota(jnp.int32, slots)[:, None] == slot_of[None, :]).astype(jnp.bfloat16)
    send_rows = jnp.dot(place, wide_rows, preferred_element_type=jnp.float32)
    send_rows = send_rows.astype(jnp.bfloat16).reshape(clusters, slot_depth, features + EXTRA)

    live_count = store_counts[lax.axis_index("store")]
    store_scale = inverse_norms(store)
    got = lax.all_to_all(send_rows, "store", split_axis=0, concat_axis=0, tiled=True)
    got = got.reshape(slots, features + EXTRA)
    rows = got[:, :features]
    position = got[:, features].astype(jnp.float32)
    taken = got[:, features + 1].astype(jnp.float32)

    active = (lax.iota(jnp.int32, crows) < live_count)[None, :]
    raw_dot = lax.dot_general(
        rows, store, (((1,), (1,)), ((), ())), preferred_element_type=jnp.float32
    )
    cosine = jnp.where(active, raw_dot * inverse_norms(rows)[:, None] * store_scale[None, :], -2.0)
    first, second = leading_pair(cosine)

    source = lax.iota(jnp.int32, slots) // slot_depth
    row_index = (
        ((source * n_batch + lax.axis_index("batch")) * rows_dev).astype(jnp.float32) + position
    )
    recency = jnp.exp(row_index * growth) * taken
    sums = jnp.stack([jnp.sum(recency * first), jnp.sum(recency)])
    sums = over_batch(sums)
    novelty = first - sums[0] / sums[1]

    expo = jnp.where(active, jnp.exp(normalized_sharpness * (cosine - first[:, None])), 0.0)
    weighted = jnp.dot(expo.astype(jnp.bfloat16), store, preferred_element_type=jnp.float32)
    near = weighted * (ROW_SCALE / jnp.sum(expo, axis=1))[:, None]

    parts = [p for v in (first, second, novelty) for p in split_parts(v)]
    parts = jnp.stack(parts + [jnp.zeros_like(parts[0])] * (EXTRA - len(parts)), axis=1)
    back = jnp.concatenate([near.astype(jnp.float16), parts], axis=1)
    back = back.reshape(n_store, slot_depth, features + EXTRA)
    back = lax.all_to_all(back, "store", split_axis=0, concat_axis=0, tiled=True)
    back = back.reshape(slots, features + EXTRA).astype(jnp.float32)

    high = lax.reduce_precision(back, 8, 7)
    low = (back - high).astype(jnp.bfloat16)
    high = high.astype(jnp.bfloat16)
    pick = (slot_of[:, None] == lax.iota(jnp.int32, slots)[None, :]).astype(jnp.bfloat16)
    mine = jnp.dot(pick, high, preferred_element_type=jnp.float32) + jnp.dot(
        pick, low, preferred_element_type=jnp.float32
    )
    neighbours = mine[:, :features] * (1.0 / ROW_SCALE)
    values = mine[:, features : features + 6 : 2] + mine[:, features + 1 : features + 6 : 2] * (
        1.0 / LOW_SCALE
    )
    return (values[:, :2], values[:, 2], neighbours)


def solution(mesh):
    in_specs = (P(("store", "batch"), None), P(("store", "batch")), P("store", None), P())
    out_specs = (P(("store", "batch"), None), P(("store", "batch")), P(("store", "batch"), None))
    return jax.shard_map(body, mesh=mesh, in_specs=in_specs, out_specs=out_specs, check_vma=False)
```

time: 150 us -> 92.4 us (0.62)
  blocking collectives: 78.8 us -> 26.9 us
  starting transfers between devices: 24.4 us -> 18 us
  waiting for transfers between devices: 19.3 us -> 15.8 us
  other arithmetic: 8.81 us -> 11.6 us
  matrix products: 7.93 us -> 9.84 us
  local copies, waits for them, and re-layouts: 9.2 us -> 7.61 us
    psum x1 -> x0, blocking collectives: 78.8 us -> none  [body(): lax.psum((jnp.sum(belonging_real * (recency * top_cos)[:, None], axis=0),...]
    all_to_all x0 -> x1, blocking collectives: none -> 26.9 us  [body(): lax.all_to_all(back, 'store', split_axis=0, concat_axis=0, tiled=True)]
    all_to_all x2 -> x0, starting transfers between devices: 11.4 us -> none  [the longest x1 5.78 us: body(): lax.all_to_all(best_slots, 'store', split_axis=0, concat_axis=0, tiled=True)]
    ppermute x0 -> x3, starting transfers between devices: none -> 5 us  [over_batch(): lax.ppermute(value, 'batch', [(i, (i + k) % n) for i in range(n)])]
    all_to_all x2 -> x0, waiting for transfers between devices: 4.81 us -> none  [the longest x1 4.81 us: body(): lax.all_to_all(best_slots, 'store', split_axis=0, concat_axis=0, tiled=True)]
    gather x2 -> x0, local copies, waits for them, and re-layouts: 2.32 us -> none  [the longest x1 1.67 us: body(): neighbours = back_near.reshape(clusters * slot_depth, features)[slot_of]]
    add x0 -> x3, other arithmetic: none -> 2.05 us  [the longest x1 1.37 us: over_batch(): total + lax.ppermute(value, 'batch', [(i, (i + k) % n) for i in range(n)])]
    dot_general x2 -> x5, matrix products: 7.93 us -> 9.84 us  [the longest x1 4.01 us: body(): lax.dot_general(rows, store, (((1,), (1,)), ((), ())), preferred_element_...]
  transfers between devices with their start and end apart: 3 -> 4, of which waited for: 2 -> 1; matrix products, arithmetic and copies ran while one was open for 8% -> 11% of each run, Pallas kernels for 0% -> 0%
where the time goes in v1:
time: 92.4 us; the launch traced here: 92 us
  blocking collectives  26.9 us (29%)
  starting transfers between devices  18 us (19%)
  waiting for transfers between devices  15.8 us (17%)
  other arithmetic  11.6 us (13%)
  matrix products  9.84 us (11%)
  local copies, waits for them, and re-layouts  7.61 us (8%)
  between operations  2.26 us (2%)
    all_to_all x1, blocking collectives, body(): lax.all_to_all(back, 'store', split_axis=0, concat_axis=0, tiled=True)  26.9 us
    all_to_all x1, waiting for transfers between devices, body(): lax.all_to_all(send_rows, 'store', split_axis=0, concat_axis=0, tiled=True)  15.8 us
    all_to_all x1, starting transfers between devices, body(): lax.all_to_all(send_rows, 'store', split_axis=0, concat_axis=0, tiled=True)  13 us
    ppermute x3, starting transfers between devices, over_batch(): lax.ppermute(value, 'batch', [(i, (i + k) % n) for i in range(n)])  5 us
    dot_general x1, matrix products, body(): lax.dot_general(rows, store, (((1,), (1,)), ((), ())), preferred_element_...  4.01 us
    dot_general x1, matrix products, body(): jnp.dot(expo.astype(jnp.bfloat16), store, preferred_element_type=jnp.floa...  3.95 us
    reduce_sum x2, other arithmetic, inverse_norms(): return lax.rsqrt(jnp.sum(wide * wide, axis=1) + epsilon)  3.52 us
  transfers between devices with their start and end apart: 4, of which 1 were waited for; matrix products, arithmetic and copies ran while one was open for 11% of the time, Pallas kernels for 0%

profile of v1, /device:TPU:1, one launch (start us, length us, event | category | flops | bytes accessed | tf_op | source)
XLA Modules:
  0.0 92.0 jit_solution(11684156699780988978)
XLA Ops:
  0.7 0.9 convert_reduce_fusion.3
  1.6 0.7 multiply_add_fusion.1
  2.3 1.3 %convolution_convert_fusion = bf16[256,1280]{1,0:T(8,128)(2,1)S(1)} fusion(bf16[128,128]{1,0:T(8,128)(2,1)S(1)} %broadcast_select_fusion, bf16[128,1152]{1,0:T(8,128)(2,1)} %param.4, s32[128]{0:T(128)S(1)} %multiply_add_fusion.1), kind=kOutput, calls=%fused_computation.7 | convolution fusion | flops 84901888 | bytes 983552 | tf_op jit(solution)/shard_map/dot_general | solution.py:68
  3.6 1.0 %reshape.198 = bf16[64,4,1280]{2,1,0:T(4,128)(2,1)} reshape(bf16[256,1280]{1,0:T(8,128)(2,1)S(1)} %convolution_convert_fusion) | data formatting | bytes 1310720 | tf_op jit(solution)/shard_map/reshape | solution.py:69
  4.6 13.0 %all-to-all-start = ((bf16[64,4,1280]{2,1,0:T(4,128)(2,1)}), bf16[64,4,1280]{2,1,0:T(4,128)(2,1)S(1)}, u32[]{:S(2)}, u32[]{:S(2)}) async-start(bf16[64,4,1280]{2,1,0:T(4,128)(2,1)} %reshape.198), calls=%async_computation | async-start | bytes 1310720 | tf_op jit(solution)/shard_map/all_to_all | solution.py:73
  17.6 0.6 dynamic_slice.3
  18.2 0.7 iota_compare_fusion.6
  18.9 3.3 %multiply_reduce_fusion = f32[2048]{0:T(1024)S(1)} fusion(bf16[2048,1152]{1,0:T(8,128)(2,1)} %param.6), kind=kLoop, calls=%fused_computation | loop fusion | flops 7075840 | bytes 4726784 | tf_op jit(solution)/shard_map/reduce_sum | solution.py:17
  22.2 15.8 %all-to-all-done = bf16[64,4,1280]{2,1,0:T(4,128)(2,1)S(1)} async-done(((bf16[64,4,1280]{2,1,0:T(4,128)(2,1)}), bf16[64,4,1280]{2,1,0:T(4,128)(2,1)S(1)}, u32[]{:S(2)}, u32[]{:S(2)}) %all-to-all-start) | async-done | bytes 655392 | tf_op jit(solution)/shard_map/all_to_all | solution.py:73
  38.1 0.2 multiply_reduce_fusion.1
  38.3 0.2 convert_reduce_fusion.2
  38.5 4.0 %fusion.41 = (f32[256]{0:T(256)S(1)}, f32[256,2048]{1,0:T(8,128)S(1)}) fusion(f32[2048]{0:T(1024)S(1)} %add_rsqrt_fusion, f32[256]{0:T(256)S(1)} %add_rsqrt_fusion.1, bf16[2048,1152]{1,0:T(8,128)(2,1)} %param.6, bf16[256,1280]{1,0:T(8,128)(2,1)S(1)} %reshape.199, pred[2048]{0:T(1024)(128)(4,1)S(1)} %iota_compare_fusion.6), kind=kOutput, calls=%fused_computation.82 | convolution fusion | flops 1210056448 | bytes 7417856 | tf_op jit(solution)/shard_map/dot_general | solution.py:80
  42.5 0.6 multiply_reduce_fusion.2
  43.1 1.4 %pad_maximum_fusion = f32[2]{0:T(128)S(1)} fusion(f32[1]{0:T(128)} %bitcast.2, f32[1]{0:T(128)} %bitcast.1), kind=kLoop, calls=%fused_computation.71 | loop fusion | flops 2 | bytes 16 | tf_op jit(solution)/shard_map/stack | solution.py:91
  44.5 1.3 %collective-permute-start = (f32[2]{0:T(128)S(1)}, f32[2]{0:T(128)S(1)}, u32[]{:S(2)}, u32[]{:S(2)}) collective-permute-start(f32[2]{0:T(128)S(1)} %pad_maximum_fusion), channel_id=1, source_target_pairs={{0,1},{1,2},{2,3},{3,0},{4,5},{5,6},{6,7},{7,4},{8,9},{9,10},{10,1... | collective-permute-start | bytes 32 | tf_op jit(solution)/shard_map/ppermute | solution.py:38
  45.8 2.6 %collective-permute-start.1 = (f32[2]{0:T(128)S(1)}, f32[2]{0:T(128)S(1)}, u32[]{:S(2)}, u32[]{:S(2)}) collective-permute-start(f32[2]{0:T(128)S(1)} %pad_maximum_fusion), channel_id=1, source_target_pairs={{0,2},{1,3},{2,0},{3,1},{4,6},{5,7},{6,4},{7,5},{8,10},{9,11},{10,... | collective-permute-start | bytes 32 | tf_op jit(solution)/shard_map/ppermute | solution.py:38
  48.5 1.1 %collective-permute-start.2 = (f32[2]{0:T(128)S(1)}, f32[2]{0:T(128)S(1)}, u32[]{:S(2)}, u32[]{:S(2)}) collective-permute-start(f32[2]{0:T(128)S(1)} %pad_maximum_fusion), channel_id=1, source_target_pairs={{0,3},{1,0},{2,1},{3,2},{4,7},{5,4},{6,5},{7,6},{8,11},{9,8},{10,9... | collective-permute-start | bytes 32 | tf_op jit(solution)/shard_map/ppermute | solution.py:38
  49.5 0.8 fusion.3
  50.3 0.4 convert_reduce_fusion
  51.2 4.0 %fusion.2 = f16[256,1152]{1,0:T(8,128)(2,1)S(1)} fusion(bf16[2048,1152]{1,0:T(8,128)(2,1)} %param.6, f32[256,2048]{1,0:T(8,128)S(1)} %get-tuple-element.33, f32[256]{0:T(256)S(1)} %get-tuple-element.32, pred[2048]{0:T(1024)(128)(4,1)S(1)} %iota_compare_fusion.6, f32[256]{0:T(256)S(1)} %broadcast_divide_fusion), kind=kOutput, calls=%fused_computation.6 | convolution fusion | flops 1210646528 | bytes 7409664 | tf_op jit(solution)/shard_map/dot_general | solution.py:96
  55.2 0.2 concatenate.25
  55.4 1.4 %add_add_fusion = f32[2]{0:T(128)S(1)} fusion(f32[2]{0:T(128)S(1)} %collective-permute-done.2, f32[2]{0:T(128)S(1)} %collective-permute-done.1, f32[2]{0:T(128)S(1)} %collective-permute-done, f32[1]{0:T(128)} %bitcast.2, f32[1]{0:T(128)} %bitcast.1), kind=kLoop, calls=%fused_computation.72 | loop fusion | flops 8 | bytes 40 | tf_op jit(solution)/shard_map/add | solution.py:38
  56.8 0.6 fusion.40
  59.8 1.5 %concatenate.31 = f16[64,4,1280]{2,1,0:T(4,128)(2,1)S(1)} concatenate(f16[64,4,1152]{2,1,0:T(4,128)(2,1)S(1)} %concatenate.25, f16[64,4,1]{2,1,0:T(4,128)(2,1)S(1)} %copy.36, f16[64,4,1]{2,1,0:T(4,128)(2,1)S(1)} %copy.37, f16[64,4,1]{2,1,0:T(4,128)(2,1)S(1)} %copy.38, f16[64,4,1]{2,1,0:T(4,128)(2,1)S(1)} %copy.39, f16[64,4,1]{2,1,0:T(4,128)(2,1)S(1)} %copy.40, ...), dimensions={2} | concatenate | bytes 1310720 | tf_op jit(solution)/shard_map/concatenate | solution.py:101
  61.4 26.9 %all_to_all.10 = f16[64,4,1280]{2,1,0:T(4,128)(2,1)S(1)} all-to-all(f16[64,4,1280]{2,1,0:T(4,128)(2,1)S(1)} %concatenate.31), channel_id=1, replica_groups=mesh['store'=64,'batch'=4] {'store'}, dimensions={0} | all-to-all | bytes 1310720 | tf_op jit(solution)/shard_map/all_to_all | solution.py:103
  88.2 0.2 convert_element_type.157
  88.5 0.5 reshape.202
  88.9 0.3 fusion.13
  89.2 0.3 convolution_add_fusion
  89.5 0.9 slice_multiply_fusion
  90.7 0.7 slice_reduce_fusion
  91.3 0.6 copy.42
  (35 shorter events, 2.1 us)
Async XLA Ops:
  0.6 17.0 %copy-start = (s32[64]{0:T(128)S(1)}, s32[64]{0:T(128)}, u32[]{:S(2)}) copy-start(s32[64]{0:T(128)} %param.7) | copy-start | bytes 772
  4.6 33.4 %all-to-all-start = ((bf16[64,4,1280]{2,1,0:T(4,128)(2,1)}), bf16[64,4,1280]{2,1,0:T(4,128)(2,1)S(1)}, u32[]{:S(2)}, u32[]{:S(2)}) async-start(bf16[64,4,1280]{2,1,0:T(4,128)(2,1)} %reshape.198), calls=%async_computation | async-start | bytes 1310720 | tf_op jit(solution)/shard_map/all_to_all | solution.py:73
  44.5 10.9 %collective-permute-start = (f32[2]{0:T(128)S(1)}, f32[2]{0:T(128)S(1)}, u32[]{:S(2)}, u32[]{:S(2)}) collective-permute-start(f32[2]{0:T(128)S(1)} %pad_maximum_fusion), channel_id=1, source_target_pairs={{0,1},{1,2},{2,3},{3,0},{4,5},{5,6},{6,7},{7,4},{8,9},{9,10},{10,1... | collective-permute-start | bytes 32 | tf_op jit(solution)/shard_map/ppermute | solution.py:38
  45.8 9.6 %collective-permute-start.1 = (f32[2]{0:T(128)S(1)}, f32[2]{0:T(128)S(1)}, u32[]{:S(2)}, u32[]{:S(2)}) collective-permute-start(f32[2]{0:T(128)S(1)} %pad_maximum_fusion), channel_id=1, source_target_pairs={{0,2},{1,3},{2,0},{3,1},{4,6},{5,7},{6,4},{7,5},{8,10},{9,11},{10,... | collective-permute-start | bytes 32 | tf_op jit(solution)/shard_map/ppermute | solution.py:38
  48.5 7.0 %collective-permute-start.2 = (f32[2]{0:T(128)S(1)}, f32[2]{0:T(128)S(1)}, u32[]{:S(2)}, u32[]{:S(2)}) collective-permute-start(f32[2]{0:T(128)S(1)} %pad_maximum_fusion), channel_id=1, source_target_pairs={{0,3},{1,0},{2,1},{3,2},{4,7},{5,4},{6,5},{7,6},{8,11},{9,8},{10,9... | collective-permute-start | bytes 32 | tf_op jit(solution)/shard_map/ppermute | solution.py:38

commit v2 on v1

v2 whole, which is shorter than its diff:
```python
import functools
import math

import jax
import jax.numpy as jnp
from jax import lax
from jax.experimental import pallas as pl
from jax.experimental.pallas import tpu as pltpu
from jax.sharding import PartitionSpec as P

normalized_sharpness = 160.0
epsilon = 1e-06
EXTRA = 128
STEPS = 32767.0
COSINE_UNIT = 16384.0
SUM_UNIT = 32.0
LOG_UNIT = 256.0
LOW_UNIT = 16384.0
TILE = 256
VMEM_BYTES = 24 * 2**20


def dot(a, b, contract):
    return lax.dot_general(a, b, ((contract[:1], contract[1:]), ((), ())), preferred_element_type=jnp.float32)


def cluster_pairs(cluster_ref):
    across = jnp.broadcast_to(cluster_ref[...], (cluster_ref.shape[1],) * 2)
    down = across.T
    i = lax.broadcasted_iota(jnp.int32, across.shape, 0)
    j = lax.broadcasted_iota(jnp.int32, across.shape, 1)
    return across, down, i, j


def place_kernel(depth, cluster_ref, queries_ref, out_ref):
    across, down, i, j = cluster_pairs(cluster_ref)
    rows, features = queries_ref.shape
    rank = jnp.sum(jnp.where((across == down) & (i < j), 1.0, 0.0), axis=0, keepdims=True)
    slot = across[:1] * depth + rank.astype(jnp.int32)
    slots = out_ref.shape[0] * depth
    place = jnp.where(lax.broadcasted_iota(jnp.int32, (slots, rows), 0) == slot, 1.0, 0.0)
    place = place.astype(jnp.bfloat16)
    tail = jnp.where(j == 0, i.astype(jnp.float32), jnp.where(j == 1, 1.0, 0.0))
    sent = dot(place, queries_ref[...], (1, 0)).astype(jnp.bfloat16)
    out_ref[:, :, :features] = sent.reshape(-1, depth, features)
    sent = dot(place, tail.astype(jnp.bfloat16), (1, 0)).astype(jnp.bfloat16)
    out_ref[:, :, features:] = sent.reshape(-1, depth, EXTRA)


def parts(value, unit):
    high = jnp.round(value * unit)
    return [high, jnp.round((value * unit - high) * LOW_UNIT)]


def score_kernel(growth, n_batch, rows_dev, info_ref, got_ref, store_ref, scale_ref, out_ref, cos_ref, expo_ref):
    sources, depth, width = got_ref.shape
    features = width - EXTRA
    slots = sources * depth
    crows = store_ref.shape[0]
    live, batch = info_ref[0], info_ref[1]
    rows = got_ref[:, :, :features].reshape(slots, features)
    tail = got_ref[:, :, features:].astype(jnp.float32).reshape(slots, EXTRA)
    wide = rows.astype(jnp.float32)
    row_scale = lax.rsqrt(jnp.sum(wide * wide, axis=1, keepdims=True) + epsilon)
    lane = lax.broadcasted_iota(jnp.int32, (slots, 128), 1)
    one = jnp.full((slots, 128), -3.0, jnp.float32)
    two = one
    for t in range(crows // TILE):
        raw = dot(rows, store_ref[t * TILE : (t + 1) * TILE, :], (1, 1))
        for h in range(TILE // 128):
            at = t * TILE + h * 128
            cosine = raw[:, h * 128 : (h + 1) * 128] * row_scale * scale_ref[:, at : at + 128]
            cosine = jnp.where(lane < live - at, cosine, -2.0)
            cos_ref[:, at : at + 128] = cosine
            two = jnp.maximum(two, jnp.minimum(one, cosine))
            one = jnp.maximum(one, cosine)
    first = jnp.max(one, axis=1, keepdims=True)
    holder = jnp.min(jnp.where(one == first, lane, 128), axis=1, keepdims=True)
    second = jnp.max(jnp.where(lane == holder, two, one), axis=1, keepdims=True)

    total = jnp.zeros((slots, 128), jnp.float32)
    for at in range(0, crows, 128):
        expo = jnp.exp(normalized_sharpness * (cos_ref[:, at : at + 128] - first))
        expo = jnp.where(lane < live - at, expo, 0.0)
        total = total + expo
        expo_ref[:, at : at + 128] = expo.astype(jnp.bfloat16)
    total = jnp.sum(total, axis=1, keepdims=True)
    weighted = dot(expo_ref[...], store_ref[...], (1, 0))
    largest = jnp.maximum(jnp.max(jnp.abs(weighted), axis=1, keepdims=True), 1e-30)
    coded = jnp.round(weighted * (STEPS / largest)).astype(jnp.int32)
    out_ref[:, :, :features] = coded.reshape(sources, depth, features).astype(jnp.int16)

    slot = lax.broadcasted_iota(jnp.int32, (slots, 1), 0)
    index = (slot // depth * n_batch + batch) * rows_dev + tail[:, :1].astype(jnp.int32)
    recency = jnp.exp(index.astype(jnp.float32) * growth) * tail[:, 1:2]
    values = (
        parts(first, COSINE_UNIT)
        + parts(second, COSINE_UNIT)
        + parts(jnp.log(largest / total), LOG_UNIT)
        + parts(jnp.sum(recency * first, axis=0, keepdims=True), SUM_UNIT)
        + parts(jnp.sum(recency, axis=0, keepdims=True), SUM_UNIT)
    )
    extra = jnp.zeros((slots, 128), jnp.float32)
    for k, value in enumerate(values):
        extra = jnp.where(lane == k, value, extra)
    out_ref[:, :, features:] = extra.astype(jnp.int32).reshape(sources, depth, EXTRA).astype(jnp.int16)


def joined(high, low, unit):
    return (high + low * (1.0 / LOW_UNIT)) * (1.0 / unit)


def pick_kernel(cluster_ref, back_ref, near_ref, best_ref):
    across, down, i, j = cluster_pairs(cluster_ref)
    clusters, depth, width = back_ref.shape
    features = width - EXTRA
    slots = clusters * depth
    rank = jnp.sum(jnp.where((across == down) & (j < i), 1.0, 0.0), axis=1, keepdims=True)
    slot = down[:, :1] * depth + rank.astype(jnp.int32)
    pick = jnp.where(lax.broadcasted_iota(jnp.int32, (i.shape[0], slots), 1) == slot, 1.0, 0.0)
    pick = pick.astype(jnp.bfloat16)

    def mine(value):
        value = value.astype(jnp.float32).reshape(slots, -1)
        high = jnp.floor(value * (1.0 / 256.0))
        low = value - high * 256.0
        return dot(pick, high.astype(jnp.bfloat16), (1, 0)) * 256.0 + dot(pick, low.astype(jnp.bfloat16), (1, 0))

    extra = mine(back_ref[:, :, features:])
    largest = jnp.exp(joined(extra[:, 4:5], extra[:, 5:6], LOG_UNIT))
    near_ref[...] = mine(back_ref[:, :, :features]) * (largest * (1.0 / STEPS))
    extra = extra.T
    best_ref[0:1, :] = joined(extra[0:1], extra[1:2], COSINE_UNIT)
    best_ref[1:2, :] = joined(extra[2:3], extra[3:4], COSINE_UNIT)


def over_batch(value):
    n = lax.axis_size("batch")
    total = value
    for k in range(1, n):
        total = total + lax.ppermute(value, "batch", [(i, (i + k) % n) for i in range(n)])
    return total


def inverse_norms(block_of):
    wide = block_of.astype(jnp.float32)
    return lax.rsqrt(jnp.sum(wide * wide, axis=1) + epsilon)


def body(queries, query_cluster, store, store_counts):
    n_store = lax.axis_size("store")
    n_batch = lax.axis_size("batch")
    rows_dev, features = queries.shape
    clusters = store_counts.shape[0]
    crows = store.shape[0]
    depth = 2 * rows_dev // clusters
    slots = clusters * depth
    width = features + EXTRA
    growth = math.log(3.0) / (rows_dev * n_store * n_batch)
    params = pltpu.CompilerParams(vmem_limit_bytes=VMEM_BYTES)

    cluster_row = query_cluster.reshape(1, rows_dev)
    send = pl.pallas_call(
        functools.partial(place_kernel, depth),
        out_shape=jax.ShapeDtypeStruct((clusters, depth, width), jnp.bfloat16),
        compiler_params=params,
    )(cluster_row, queries)

    info = jnp.stack([store_counts[lax.axis_index("store")], lax.axis_index("batch")])
    store_scale = inverse_norms(store).reshape(1, crows)
    got = lax.all_to_all(send, "store", split_axis=0, concat_axis=0, tiled=True)

    vmem = pl.BlockSpec(memory_space=pltpu.VMEM)
    back = pl.pallas_call(
        functools.partial(score_kernel, growth, n_batch, rows_dev),
        out_shape=jax.ShapeDtypeStruct((n_store, depth, width), jnp.int16),
        in_specs=[pl.BlockSpec(memory_space=pltpu.SMEM), vmem, vmem, vmem],
        out_specs=vmem,
        scratch_shapes=[pltpu.VMEM((slots, crows), jnp.float32), pltpu.VMEM((slots, crows), jnp.bfloat16)],
        compiler_params=params,
    )(info, got, store, store_scale)
    back = lax.all_to_all(back, "store", split_axis=0, concat_axis=0, tiled=True)

    sums = back[:, 0, features + 6 : features + 10].astype(jnp.float32)
    sums = over_batch(joined(sums[:, 0::2], sums[:, 1::2], SUM_UNIT))
    near, best = pl.pallas_call(
        pick_kernel,
        out_shape=(
            jax.ShapeDtypeStruct((rows_dev, features), jnp.float32),
            jax.ShapeDtypeStruct((2, rows_dev), jnp.float32),
        ),
        compiler_params=params,
    )(cluster_row, back)
    mean = sums[:, 0] / sums[:, 1]
    member = query_cluster[:, None] == lax.iota(jnp.int32, clusters)[None, :]
    novelty = best[0] - jnp.sum(jnp.where(member, mean[None, :], 0.0), axis=1)
    return (best.T, novelty, near)


def solution(mesh):
    in_specs = (P(("store", "batch"), None), P(("store", "batch")), P("store", None), P())
    out_specs = (P(("store", "batch"), None), P(("store", "batch")), P(("store", "batch"), None))
    return jax.shard_map(body, mesh=mesh, in_specs=in_specs, out_specs=out_specs, check_vma=False)
```

time: 92.4 us -> 79.5 us (0.86)
  matrix products: 9.84 us -> 0 us
  Pallas kernels: 0 us -> 7.53 us
  other arithmetic: 11.6 us -> 5.67 us
  local copies, waits for them, and re-layouts: 7.61 us -> 5.36 us
  between operations: 2.26 us -> 0.72 us
    dot_general x5 -> x0, matrix products: 9.84 us -> none  [the longest x1 4.01 us: body(): lax.dot_general(rows, store, (((1,), (1,)), ((), ())), preferred_element_...]
    pallas_call x0 -> x3, Pallas kernels: none -> 7.53 us  [the longest x1 4.63 us: body(): pl.pallas_call(functools.partial(score_kernel, growth, n_batch, rows_dev)...]
    unnamed x3 -> x8, local copies, waits for them, and re-layouts: 0.64 us -> 3.95 us
    concatenate x7 -> x0, local copies, waits for them, and re-layouts: 1.84 us -> none  [body(): back = jnp.concatenate([near.astype(jnp.float16), parts], axis=1)]
    reduce_sum x3 -> x1, other arithmetic: 1.9 us -> 0.09 us  [body(): novelty = best[0] - jnp.sum(jnp.where(member, mean[None, :], 0.0), axis=1)]
    add x1, other arithmetic: 1.37 us -> 0.01 us  [over_batch(): total + lax.ppermute(value, 'batch', [(i, (i + k) % n) for i in range(n)])]
    slice x4 -> x2, local copies, waits for them, and re-layouts: 1.51 us -> 0.17 us  [body(): sums = over_batch(joined(sums[:, 0::2], sums[:, 1::2], SUM_UNIT))]
    convert_element_type x7 -> x0, local copies, waits for them, and re-layouts: 1.33 us -> none  [the longest x6 0.88 us: split_parts(): return (high.astype(jnp.float16), low.astype(jnp.float16))]
  transfers between devices with their start and end apart: 4 -> 4, of which waited for: 1 -> 2; matrix products, arithmetic and copies ran while one was open for 11% -> 7% of each run, Pallas kernels for 0% -> 2%
where the time goes in v2:
time: 79.5 us; the launch traced here: 78.7 us
  blocking collectives  26 us (33%)
  starting transfers between devices  18.1 us (23%)
  waiting for transfers between devices  15.4 us (19%)
  Pallas kernels  7.53 us (9%)
  other arithmetic  5.67 us (7%)
  local copies, waits for them, and re-layouts  5.36 us (7%)
    all_to_all x1, blocking collectives, body(): lax.all_to_all(back, 'store', split_axis=0, concat_axis=0, tiled=True)  26 us
    all_to_all x1, waiting for transfers between devices, body(): got = lax.all_to_all(send, 'store', split_axis=0, concat_axis=0, tiled=True)  15 us
    all_to_all x1, starting transfers between devices, body(): got = lax.all_to_all(send, 'store', split_axis=0, concat_axis=0, tiled=True)  13 us
    ppermute x3, starting transfers between devices, over_batch(): lax.ppermute(value, 'batch', [(i, (i + k) % n) for i in range(n)])  5.07 us
    pallas_call x1, Pallas kernels, body(): pl.pallas_call(functools.partial(score_kernel, growth, n_batch, rows_dev)...  4.63 us
    unnamed x8, local copies, waits for them, and re-layouts  3.95 us
    reduce_sum x1, other arithmetic, inverse_norms(): return lax.rsqrt(jnp.sum(wide * wide, axis=1) + epsilon)  3.32 us
    pallas_call x1, Pallas kernels, body(): pl.pallas_call(pick_kernel, out_shape=(jax.ShapeDtypeStruct((rows_dev, fe...  1.64 us
  transfers between devices with their start and end apart: 4, of which 2 were waited for; matrix products, arithmetic and copies ran while one was open for 7% of the time, Pallas kernels for 2%

profile of v2, /device:TPU:1, one launch (start us, length us, event | category | flops | bytes accessed | tf_op | source)
XLA Modules:
  0.0 78.7 jit_solution(10202737381466579068)
XLA Ops:
  0.6 0.0 copy-start.1
  0.6 1.0 %copy-done.1 = bf16[128,1152]{1,0:T(8,128)(2,1)S(1)} copy-done((bf16[128,1152]{1,0:T(8,128)(2,1)S(1)}, bf16[128,1152]{1,0:T(8,128)(2,1)}, u32[]{:S(2)}) %copy-start.1) | copy-done | bytes 294936
  1.6 0.0 copy-start.2
  1.6 0.7 copy-done.2
  2.2 1.3 %shard_map.67 = bf16[64,4,1280]{2,1,0:T(4,128)(2,1)} custom-call(s32[1,128]{1,0:T(1,128)S(1)} %bitcast.8, bf16[128,1152]{1,0:T(8,128)(2,1)S(1)} %copy-done.1), custom_call_target="tpu_custom_call" | custom-call | tf_op jit(solution)/shard_map/pallas_call | solution.py:163
  3.5 13.0 %all-to-all-start = ((bf16[64,4,1280]{2,1,0:T(4,128)(2,1)}), bf16[64,4,1280]{2,1,0:T(4,128)(2,1)S(1)}, u32[]{:S(2)}, u32[]{:S(2)}) async-start(bf16[64,4,1280]{2,1,0:T(4,128)(2,1)} %shard_map.67), calls=%async_computation | async-start | bytes 1310720 | tf_op jit(solution)/shard_map/all_to_all | solution.py:171
  16.5 1.2 %dynamic_slice.3 = s32[1]{0:T(128)} dynamic-slice(s32[64]{0:T(128)} %param.7, s32[]{:T(128)S(6)} %select_n.7), dynamic_slice_sizes={1} | dynamic-slice | bytes 12 | tf_op jit(solution)/shard_map/dynamic_slice | solution.py:169
  17.8 0.7 pad_add_fusion.info_ref
  18.5 3.3 %multiply_reduce_fusion = f32[2048]{0:T(1024)S(1)} fusion(bf16[2048,1152]{1,0:T(8,128)(2,1)} %store_ref.1), kind=kLoop, calls=%fused_computation | loop fusion | flops 7075840 | bytes 4726784 | tf_op jit(solution)/shard_map/reduce_sum | solution.py:147
  21.8 0.0 copy-start.3
  21.8 15.0 %all-to-all-done.got_ref = bf16[64,4,1280]{2,1,0:T(4,128)(2,1)S(1)} async-done(((bf16[64,4,1280]{2,1,0:T(4,128)(2,1)}), bf16[64,4,1280]{2,1,0:T(4,128)(2,1)S(1)}, u32[]{:S(2)}, u32[]{:S(2)}) %all-to-all-start) | async-done | bytes 655392 | tf_op jit(solution)/shard_map/all_to_all | solution.py:171
  36.9 0.0 copy-start
  36.9 2.3 %copy-done = bf16[2048,1152]{1,0:T(8,128)(2,1)S(1)} copy-done((bf16[2048,1152]{1,0:T(8,128)(2,1)S(1)}, bf16[2048,1152]{1,0:T(8,128)(2,1)}, u32[]{:S(2)}) %copy-start) | copy-done | bytes 4718616
  39.2 4.6 %shard_map.68 = s16[64,4,1280]{2,1,0:T(4,128)(2,1)S(1)} custom-call(s32[2]{0:T(128)S(1)} %pad_add_fusion.info_ref, bf16[64,4,1280]{2,1,0:T(4,128)(2,1)S(1)} %all-to-all-done.got_ref, bf16[2048,1152]{1,0:T(8,128)(2,1)S(1)} %copy-done, f32[1,2048]{1,0:T(1,128)S(1)} %bitcast.7), custom_call_target="tpu_custom_call" | custom-call | tf_op jit(solution)/shard_map/pallas_call | solution.py:174
  43.8 26.0 %all_to_all.10.back_ref = s16[64,4,1280]{2,1,0:T(4,128)(2,1)S(1)} all-to-all(s16[64,4,1280]{2,1,0:T(4,128)(2,1)S(1)} %shard_map.68), channel_id=1, replica_groups=mesh['store'=64,'batch'=4] {'store'}, dimensions={0} | all-to-all | bytes 1310720 | tf_op jit(solution)/shard_map/all_to_all | solution.py:182
  69.9 0.1 slice_convert_fusion
  70.0 0.1 slice.20
  70.1 0.1 slice.21
  70.2 1.4 %collective-permute-start = (f32[64,2]{1,0:T(8,128)S(1)}, f32[64,2]{1,0:T(8,128)S(1)}, u32[]{:S(2)}, u32[]{:S(2)}) collective-permute-start(f32[64,2]{1,0:T(8,128)S(1)} %add_multiply_fusion), channel_id=1, source_target_pairs={{0,1},{1,2},{2,3},{3,0},{4,5},{5,6},{6,7},{7,4},{8,9},{9,10},{10,1... | collective-permute-start | bytes 1544 | tf_op jit(solution)/shard_map/ppermute | solution.py:141
  71.6 2.6 %collective-permute-start.1 = (f32[64,2]{1,0:T(8,128)S(1)}, f32[64,2]{1,0:T(8,128)S(1)}, u32[]{:S(2)}, u32[]{:S(2)}) collective-permute-start(f32[64,2]{1,0:T(8,128)S(1)} %add_multiply_fusion), channel_id=1, source_target_pairs={{0,2},{1,3},{2,0},{3,1},{4,6},{5,7},{6,4},{7,5},{8,10},{9,11},{10,... | collective-permute-start | bytes 1544 | tf_op jit(solution)/shard_map/ppermute | solution.py:141
  74.2 1.1 %collective-permute-start.2 = (f32[64,2]{1,0:T(8,128)S(1)}, f32[64,2]{1,0:T(8,128)S(1)}, u32[]{:S(2)}, u32[]{:S(2)}) collective-permute-start(f32[64,2]{1,0:T(8,128)S(1)} %add_multiply_fusion), channel_id=1, source_target_pairs={{0,3},{1,0},{2,1},{3,2},{4,7},{5,4},{6,5},{7,6},{8,11},{9,8},{10,9... | collective-permute-start | bytes 1544 | tf_op jit(solution)/shard_map/ppermute | solution.py:141
  75.3 0.0 copy-done.3
  75.3 1.6 %shard_map.69 = (f32[128,1152]{1,0:T(8,128)}, f32[2,128]{1,0:T(2,128)}) custom-call(s32[1,128]{1,0:T(1,128)S(1)} %bitcast.9, s16[64,4,1280]{2,1,0:T(4,128)(2,1)S(1)} %all_to_all.10.back_ref), custom_call_target="tpu_custom_call" | custom-call | tf_op jit(solution)/shard_map/pallas_call | solution.py:186
  76.9 0.0 collective-permute-done
  76.9 0.0 collective-permute-done.1
  76.9 0.3 collective-permute-done.2
  77.3 0.2 fusion
  77.4 0.1 select_reduce_fusion
  77.5 1.2 %bitcast_subtract_fusion = f32[128]{0:T(128)} fusion(f32[128]{0:T(128)S(1)} %select_reduce_fusion, f32[2,128]{1,0:T(2,128)} %get-tuple-element.5), kind=kLoop, calls=%fused_computation.10 | loop fusion | flops 128 | bytes 1536 | tf_op jit(solution)/shard_map/sub | solution.py:196
  (3 shorter events, 0.0 us)
Async XLA Ops:
  0.6 1.0 %copy-start.1 = (bf16[128,1152]{1,0:T(8,128)(2,1)S(1)}, bf16[128,1152]{1,0:T(8,128)(2,1)}, u32[]{:S(2)}) copy-start(bf16[128,1152]{1,0:T(8,128)(2,1)} %queries_ref.1) | copy-start | bytes 884740
  1.6 0.7 copy-start.2
  3.5 33.4 %all-to-all-start = ((bf16[64,4,1280]{2,1,0:T(4,128)(2,1)}), bf16[64,4,1280]{2,1,0:T(4,128)(2,1)S(1)}, u32[]{:S(2)}, u32[]{:S(2)}) async-start(bf16[64,4,1280]{2,1,0:T(4,128)(2,1)} %shard_map.67), calls=%async_computation | async-start | bytes 1310720 | tf_op jit(solution)/shard_map/all_to_all | solution.py:171
  21.8 53.5 %copy-start.3 = (s32[128]{0:T(128)S(1)}, s32[128]{0:T(128)}, u32[]{:S(2)}) copy-start(s32[128]{0:T(128)} %param.5) | copy-start | bytes 1540
  36.9 2.3 %copy-start = (bf16[2048,1152]{1,0:T(8,128)(2,1)S(1)}, bf16[2048,1152]{1,0:T(8,128)(2,1)}, u32[]{:S(2)}) copy-start(bf16[2048,1152]{1,0:T(8,128)(2,1)} %store_ref.1) | copy-start | bytes 14155780
  70.2 6.7 %collective-permute-start = (f32[64,2]{1,0:T(8,128)S(1)}, f32[64,2]{1,0:T(8,128)S(1)}, u32[]{:S(2)}, u32[]{:S(2)}) collective-permute-start(f32[64,2]{1,0:T(8,128)S(1)} %add_multiply_fusion), channel_id=1, source_target_pairs={{0,1},{1,2},{2,3},{3,0},{4,5},{5,6},{6,7},{7,4},{8,9},{9,10},{10,1... | collective-permute-start | bytes 1544 | tf_op jit(solution)/shard_map/ppermute | solution.py:141
  71.6 5.4 %collective-permute-start.1 = (f32[64,2]{1,0:T(8,128)S(1)}, f32[64,2]{1,0:T(8,128)S(1)}, u32[]{:S(2)}, u32[]{:S(2)}) collective-permute-start(f32[64,2]{1,0:T(8,128)S(1)} %add_multiply_fusion), channel_id=1, source_target_pairs={{0,2},{1,3},{2,0},{3,1},{4,6},{5,7},{6,4},{7,5},{8,10},{9,11},{10,... | collective-permute-start | bytes 1544 | tf_op jit(solution)/shard_map/ppermute | solution.py:141
  74.2 3.1 %collective-permute-start.2 = (f32[64,2]{1,0:T(8,128)S(1)}, f32[64,2]{1,0:T(8,128)S(1)}, u32[]{:S(2)}, u32[]{:S(2)}) collective-permute-start(f32[64,2]{1,0:T(8,128)S(1)} %add_multiply_fusion), channel_id=1, source_target_pairs={{0,3},{1,0},{2,1},{3,2},{4,7},{5,4},{6,5},{7,6},{8,11},{9,8},{10,9... | collective-permute-start | bytes 1544 | tf_op jit(solution)/shard_map/ppermute | solution.py:141

commit v3 on v2

v3 whole, which is shorter than its diff:
```python
import functools
import math

import jax
import jax.numpy as jnp
from jax import lax
from jax.experimental import pallas as pl
from jax.experimental.pallas import tpu as pltpu
from jax.sharding import PartitionSpec as P

normalized_sharpness = 160.0
epsilon = 1e-06
EXTRA = 128
STEPS = 32767.0
COSINE_UNIT = 16384.0
NOVELTY_UNIT = 8192.0
LOG_UNIT = 256.0
LOW_UNIT = 16384.0
TILE = 256
VMEM_BYTES = 24 * 2**20


def dot(a, b, contract):
    return lax.dot_general(a, b, ((contract[:1], contract[1:]), ((), ())), preferred_element_type=jnp.float32)


def cluster_pairs(cluster_ref):
    across = jnp.broadcast_to(cluster_ref[...], (cluster_ref.shape[1],) * 2)
    down = across.T
    i = lax.broadcasted_iota(jnp.int32, across.shape, 0)
    j = lax.broadcasted_iota(jnp.int32, across.shape, 1)
    return across, down, i, j


def place_kernel(depth, cluster_hbm, queries_hbm, out_ref, cluster_ref, queries_ref, cluster_sem, queries_sem):
    copy_cluster = pltpu.make_async_copy(cluster_hbm, cluster_ref, cluster_sem)
    copy_queries = pltpu.make_async_copy(queries_hbm, queries_ref, queries_sem)
    copy_cluster.start()
    copy_queries.start()
    copy_cluster.wait()
    across, down, i, j = cluster_pairs(cluster_ref)
    rows, features = queries_ref.shape
    rank = jnp.sum(jnp.where((across == down) & (i < j), 1.0, 0.0), axis=0, keepdims=True)
    slot = across[:1] * depth + rank.astype(jnp.int32)
    slots = out_ref.shape[0] * depth
    place = jnp.where(lax.broadcasted_iota(jnp.int32, (slots, rows), 0) == slot, 1.0, 0.0)
    place = place.astype(jnp.bfloat16)
    tail = jnp.where(j == 0, i.astype(jnp.float32), jnp.where(j == 1, 1.0, 0.0))
    sent = dot(place, tail.astype(jnp.bfloat16), (1, 0)).astype(jnp.bfloat16)
    out_ref[:, :, features:] = sent.reshape(-1, depth, EXTRA)
    copy_queries.wait()
    sent = dot(place, queries_ref[...], (1, 0)).astype(jnp.bfloat16)
    out_ref[:, :, :features] = sent.reshape(-1, depth, features)


def scale_kernel(store_hbm, scale_ref, near_ref, rest_ref, near_sem, rest_sem):
    near = near_ref.shape[0]
    copies = [
        pltpu.make_async_copy(store_hbm.at[pl.ds(0, near)], near_ref, near_sem),
        pltpu.make_async_copy(store_hbm.at[pl.ds(near, rest_ref.shape[0])], rest_ref, rest_sem),
    ]
    for copy in copies:
        copy.start()
    for copy, held, base in zip(copies, (near_ref, rest_ref), (0, near)):
        copy.wait()
        for at in range(0, held.shape[0], 128):
            wide = held[at : at + 128, :].astype(jnp.float32)
            wide = wide * wide
            total = wide[:, :128]
            for k in range(128, wide.shape[1], 128):
                total = total + wide[:, k : k + 128]
            total = jnp.sum(total.T, axis=0, keepdims=True)
            scale_ref[:, base + at : base + at + 128] = lax.rsqrt(total + epsilon)


def parts(value, unit):
    high = jnp.round(value * unit)
    return [high, jnp.round((value * unit - high) * LOW_UNIT)]


def cosines(rows, row_scale, held_ref, scale_ref, live, base, one, two, cos_ref):
    lane = lax.broadcasted_iota(jnp.int32, one.shape, 1)
    for t in range(0, held_ref.shape[0], TILE):
        raw = dot(rows, held_ref[t : t + TILE, :], (1, 1))
        for h in range(0, TILE, 128):
            at = t + h
            cosine = raw[:, h : h + 128] * row_scale * scale_ref[:, base + at : base + at + 128]
            cosine = jnp.where(lane < live - base - at, cosine, -2.0)
            cos_ref[:, at : at + 128] = cosine
            two = jnp.maximum(two, jnp.minimum(one, cosine))
            one = jnp.maximum(one, cosine)
    return one, two


def near_kernel(info_ref, got_ref, near_ref, scale_ref, cos_ref, rows_ref, state_ref):
    sources, depth, width = got_ref.shape
    slots, features = sources * depth, width - EXTRA
    rows_ref[...] = got_ref[...].reshape(slots, width)
    rows = rows_ref[:, :features]
    wide = rows.astype(jnp.float32)
    row_scale = lax.rsqrt(jnp.sum(wide * wide, axis=1, keepdims=True) + epsilon)
    state_ref[0] = jnp.broadcast_to(row_scale, (slots, 128))
    one = jnp.full((slots, 128), -3.0, jnp.float32)
    state_ref[1], state_ref[2] = cosines(rows, row_scale, near_ref, scale_ref, info_ref[0], 0, one, one, cos_ref)


def rest_kernel(
    growth, n_batch, rows_dev, depth, info_ref, rows_ref, state_ref, rest_ref, scale_ref, cos_ref, best_ref, sums_ref
):
    slots, width = rows_ref.shape
    features = width - EXTRA
    live, batch = info_ref[0], info_ref[1]
    tail = rows_ref[:, features:].astype(jnp.float32)
    slot = lax.broadcasted_iota(jnp.int32, (slots, 1), 0)
    index = (slot // depth * n_batch + batch) * rows_dev + tail[:, :1].astype(jnp.int32)
    recency = jnp.exp(index.astype(jnp.float32) * growth) * tail[:, 1:2]
    base = scale_ref.shape[1] - rest_ref.shape[0]
    one, two = cosines(
        rows_ref[:, :features], state_ref[0][:, :1], rest_ref, scale_ref, live, base, state_ref[1], state_ref[2], cos_ref
    )
    lane = lax.broadcasted_iota(jnp.int32, (slots, 128), 1)
    first = jnp.max(one, axis=1, keepdims=True)
    holder = jnp.min(jnp.where(one == first, lane, 128), axis=1, keepdims=True)
    second = jnp.max(jnp.where(lane == holder, two, one), axis=1, keepdims=True)
    best_ref[...] = jnp.where(lane == 0, first, second)
    across = lax.broadcasted_iota(jnp.int32, sums_ref.shape, 1)
    sums_ref[...] = jnp.where(
        across == 0,
        jnp.sum(recency * first, axis=0, keepdims=True),
        jnp.sum(recency, axis=0, keepdims=True),
    )


def weigh_kernel(info_ref, cos_near_ref, cos_rest_ref, best_ref, near_ref, rest_ref, weighted_ref, total_ref, expo_ref):
    slots, near = cos_near_ref.shape
    live = info_ref[0]
    first = best_ref[:, :1]
    lane = lax.broadcasted_iota(jnp.int32, (slots, 128), 1)
    total = jnp.zeros((slots, 128), jnp.float32)
    for cos_ref, base in ((cos_near_ref, 0), (cos_rest_ref, near)):
        for at in range(0, cos_ref.shape[1], 128):
            expo = jnp.exp(normalized_sharpness * (cos_ref[:, at : at + 128] - first))
            expo = jnp.where(lane < live - base - at, expo, 0.0)
            total = total + expo
            expo_ref[:, base + at : base + at + 128] = expo.astype(jnp.bfloat16)
    total_ref[...] = total
    weighted = dot(expo_ref[:, :near], near_ref[...], (1, 0))
    weighted_ref[...] = weighted + dot(expo_ref[:, near:], rest_ref[...], (1, 0))


def code_kernel(weighted_ref, total_ref, best_ref, *refs):
    *sums_refs, out_ref = refs
    sources, depth, width = out_ref.shape
    features = width - EXTRA
    slots = sources * depth
    sums = sums_refs[0][...]
    for ref in sums_refs[1:]:
        sums = sums + ref[...]
    mean = sums[:, :1] / sums[:, 1:2]
    first, second = best_ref[:, :1], best_ref[:, 1:2]
    total = jnp.sum(total_ref[...], axis=1, keepdims=True)
    weighted = weighted_ref[...]
    largest = jnp.maximum(jnp.max(jnp.abs(weighted), axis=1, keepdims=True), 1e-30)
    coded = jnp.round(weighted * (STEPS / largest)).astype(jnp.int32)
    out_ref[:, :, :features] = coded.reshape(sources, depth, features).astype(jnp.int16)
    values = (
        parts(first, COSINE_UNIT)
        + parts(second, COSINE_UNIT)
        + parts(jnp.log(largest / total), LOG_UNIT)
        + parts(first - mean, NOVELTY_UNIT)
    )
    lane = lax.broadcasted_iota(jnp.int32, (slots, 128), 1)
    extra = jnp.zeros((slots, 128), jnp.float32)
    for k, value in enumerate(values):
        extra = jnp.where(lane == k, value, extra)
    out_ref[:, :, features:] = extra.astype(jnp.int32).reshape(sources, depth, EXTRA).astype(jnp.int16)


def joined(high, low, unit):
    return (high + low * (1.0 / LOW_UNIT)) * (1.0 / unit)


def pick_kernel(cluster_ref, back_ref, near_ref, best_ref, novelty_ref):
    across, down, i, j = cluster_pairs(cluster_ref)
    clusters, depth, width = back_ref.shape
    features = width - EXTRA
    slots = clusters * depth
    rank = jnp.sum(jnp.where((across == down) & (j < i), 1.0, 0.0), axis=1, keepdims=True)
    slot = down[:, :1] * depth + rank.astype(jnp.int32)
    pick = jnp.where(lax.broadcasted_iota(jnp.int32, (i.shape[0], slots), 1) == slot, 1.0, 0.0)
    pick = pick.astype(jnp.bfloat16)

    def mine(value):
        value = value.astype(jnp.float32).reshape(slots, -1)
        high = jnp.floor(value * (1.0 / 256.0))
        low = value - high * 256.0
        return dot(pick, high.astype(jnp.bfloat16), (1, 0)) * 256.0 + dot(pick, low.astype(jnp.bfloat16), (1, 0))

    extra = mine(back_ref[:, :, features:])
    largest = jnp.exp(joined(extra[:, 4:5], extra[:, 5:6], LOG_UNIT))
    near_ref[...] = mine(back_ref[:, :, :features]) * (largest * (1.0 / STEPS))
    extra = extra.T
    best_ref[0:1, :] = joined(extra[0:1], extra[1:2], COSINE_UNIT)
    best_ref[1:2, :] = joined(extra[2:3], extra[3:4], COSINE_UNIT)
    novelty_ref[...] = joined(extra[6:7], extra[7:8], NOVELTY_UNIT)


def over_batch(value):
    n = lax.axis_size("batch")
    return [value] + [lax.ppermute(value, "batch", [(i, (i + k) % n) for i in range(n)]) for k in range(1, n)]


def body(queries, query_cluster, store, store_counts):
    n_store = lax.axis_size("store")
    n_batch = lax.axis_size("batch")
    rows_dev, features = queries.shape
    clusters = store_counts.shape[0]
    crows = store.shape[0]
    depth = 2 * rows_dev // clusters
    slots = clusters * depth
    width = features + EXTRA
    growth = math.log(3.0) / (rows_dev * n_store * n_batch)
    params = pltpu.CompilerParams(vmem_limit_bytes=VMEM_BYTES)

    cluster_row = query_cluster.reshape(1, rows_dev)
    send = pl.pallas_call(
        functools.partial(place_kernel, depth),
        out_shape=jax.ShapeDtypeStruct((clusters, depth, width), jnp.bfloat16),
        in_specs=[pl.BlockSpec(memory_space=pltpu.HBM)] * 2,
        scratch_shapes=[
            pltpu.VMEM((1, rows_dev), jnp.int32),
            pltpu.VMEM((rows_dev, features), jnp.bfloat16),
            pltpu.SemaphoreType.DMA,
            pltpu.SemaphoreType.DMA,
        ],
        compiler_params=pltpu.CompilerParams(vmem_limit_bytes=60 * 2**20),
    )(cluster_row, queries)

    info = jnp.stack([store_counts[lax.axis_index("store")], lax.axis_index("batch")])
    near = crows // 2
    f32, bf16 = jnp.float32, store.dtype
    vmem = pl.BlockSpec(memory_space=pltpu.VMEM)
    hbm = pl.BlockSpec(memory_space=pltpu.HBM)
    smem = pl.BlockSpec(memory_space=pltpu.SMEM)
    store_scale, store_near, store_rest = pl.pallas_call(
        scale_kernel,
        out_shape=(
            jax.ShapeDtypeStruct((1, crows), f32),
            jax.ShapeDtypeStruct((near, features), bf16),
            jax.ShapeDtypeStruct((crows - near, features), bf16),
        ),
        in_specs=[hbm],
        out_specs=(vmem,) * 3,
        scratch_shapes=[pltpu.SemaphoreType.DMA, pltpu.SemaphoreType.DMA],
        compiler_params=params,
        cost_estimate=pl.CostEstimate(flops=2 * crows * features, bytes_accessed=2 * crows * features, transcendentals=crows),
    )(store)
    got = lax.all_to_all(send, "store", split_axis=0, concat_axis=0, tiled=True)

    half_cost = pl.CostEstimate(flops=slots * crows * features, bytes_accessed=crows * features, transcendentals=0)
    cos_near, rows, state = pl.pallas_call(
        near_kernel,
        out_shape=(
            jax.ShapeDtypeStruct((slots, near), f32),
            jax.ShapeDtypeStruct((slots, width), bf16),
            jax.ShapeDtypeStruct((3, slots, 128), f32),
        ),
        in_specs=[smem, vmem, vmem, vmem],
        out_specs=(vmem,) * 3,
        compiler_params=params,
        cost_estimate=half_cost,
    )(info, got, store_near, store_scale)
    cos_rest, best, sums = pl.pallas_call(
        functools.partial(rest_kernel, growth, n_batch, rows_dev, depth),
        out_shape=(
            jax.ShapeDtypeStruct((slots, crows - near), f32),
            jax.ShapeDtypeStruct((slots, 128), f32),
            jax.ShapeDtypeStruct((1, 128), f32),
        ),
        in_specs=[smem, vmem, vmem, vmem, vmem],
        out_specs=(vmem,) * 3,
        compiler_params=params,
        cost_estimate=half_cost,
    )(info, rows, state, store_rest, store_scale)
    sums = over_batch(sums)
    weighted, total = pl.pallas_call(
        weigh_kernel,
        out_shape=(
            jax.ShapeDtypeStruct((slots, features), jnp.float32),
            jax.ShapeDtypeStruct((slots, 128), jnp.float32),
        ),
        in_specs=[smem] + [vmem] * 5,
        out_specs=(vmem, vmem),
        scratch_shapes=[pltpu.VMEM((slots, crows), jnp.bfloat16)],
        compiler_params=params,
        cost_estimate=pl.CostEstimate(flops=4 * slots * crows * features, bytes_accessed=8 * crows * features, transcendentals=slots * crows),
    )(info, cos_near, cos_rest, best, store_near, store_rest)
    back = pl.pallas_call(
        code_kernel,
        out_shape=jax.ShapeDtypeStruct((n_store, depth, width), jnp.int16),
        in_specs=[vmem] * (3 + n_batch),
        out_specs=vmem,
        compiler_params=params,
    )(weighted, total, best, *sums)
    back = lax.all_to_all(back, "store", split_axis=0, concat_axis=0, tiled=True)

    neighbours, best, novelty = pl.pallas_call(
        pick_kernel,
        out_shape=(
            jax.ShapeDtypeStruct((rows_dev, features), jnp.float32),
            jax.ShapeDtypeStruct((2, rows_dev), jnp.float32),
            jax.ShapeDtypeStruct((1, rows_dev), jnp.float32),
        ),
        compiler_params=params,
    )(cluster_row, back)
    return (best.T, novelty[0], neighbours)


def solution(mesh):
    in_specs = (P(("store", "batch"), None), P(("store", "batch")), P("store", None), P())
    out_specs = (P(("store", "batch"), None), P(("store", "batch")), P(("store", "batch"), None))
    return jax.shard_map(body, mesh=mesh, in_specs=in_specs, out_specs=out_specs, check_vma=False)
```

time: 79.5 us -> 76.7 us (0.965)
  other arithmetic: 5.67 us -> 0.72 us
  Pallas kernels: 7.53 us -> 11.4 us
  blocking collectives: 26 us -> 27.7 us
  waiting for transfers between devices: 15.4 us -> 13.9 us
  starting transfers between devices: 18.1 us -> 16.8 us
    reduce_sum x2 -> x0, other arithmetic: 3.42 us -> none  [the longest x1 3.32 us: inverse_norms(): return lax.rsqrt(jnp.sum(wide * wide, axis=1) + epsilon)]
    pallas_call x1 -> x5, Pallas kernels: 4.63 us -> 7.62 us  [the longest x1 2.24 us: body(): pl.pallas_call(weigh_kernel, out_shape=(jax.ShapeDtypeStruct((slots, feat...]
    all_to_all x1, waiting for transfers between devices: 15 us -> 13.2 us  [body(): got = lax.all_to_all(send, 'store', split_axis=0, concat_axis=0, tiled=True)]
    all_to_all x1, blocking collectives: 26 us -> 27.7 us  [body(): lax.all_to_all(back, 'store', split_axis=0, concat_axis=0, tiled=True)]
    ppermute x3, starting transfers between devices: 5.07 us -> 3.85 us  [over_batch(): lax.ppermute(value, 'batch', [(i, (i + k) % n) for i in range(n)])]
    sub x1 -> x0, other arithmetic: 1.2 us -> none  [body(): novelty = best[0] - jnp.sum(jnp.where(member, mean[None, :], 0.0), axis=1)]
    pallas_call x1, Pallas kernels: 1.26 us -> 2.16 us  [body(): pl.pallas_call(functools.partial(place_kernel, depth), out_shape=jax.Shap...]
  transfers between devices with their start and end apart: 4 -> 4, of which waited for: 2 -> 3; matrix products, arithmetic and copies ran while one was open for 7% -> 3% of each run, Pallas kernels for 2% -> 5%
where the time goes in v3:
time: 76.7 us; the launch traced here: 76.4 us
  blocking collectives  27.7 us (36%)
  starting transfers between devices  16.8 us (22%)
  waiting for transfers between devices  13.9 us (18%)
  Pallas kernels  11.4 us (15%)
  local copies, waits for them, and re-layouts  5.12 us (7%)
    all_to_all x1, blocking collectives, body(): lax.all_to_all(back, 'store', split_axis=0, concat_axis=0, tiled=True)  27.7 us
    all_to_all x1, waiting for transfers between devices, body(): got = lax.all_to_all(send, 'store', split_axis=0, concat_axis=0, tiled=True)  13.2 us
    all_to_all x1, starting transfers between devices, body(): got = lax.all_to_all(send, 'store', split_axis=0, concat_axis=0, tiled=True)  13 us
    unnamed x8, local copies, waits for them, and re-layouts  3.88 us
    ppermute x3, starting transfers between devices, over_batch(): lax.ppermute(value, 'batch', [(i, (i + k) % n) for i in range(n)])  3.85 us
    pallas_call x1, Pallas kernels, body(): pl.pallas_call(weigh_kernel, out_shape=(jax.ShapeDtypeStruct((slots, feat...  2.24 us
    pallas_call x1, Pallas kernels, body(): pl.pallas_call(functools.partial(place_kernel, depth), out_shape=jax.Shap...  2.16 us
    pallas_call x1, Pallas kernels, body(): pl.pallas_call(functools.partial(rest_kernel, growth, n_batch, rows_dev,...  1.79 us
  transfers between devices with their start and end apart: 4, of which 3 were waited for; matrix products, arithmetic and copies ran while one was open for 3% of the time, Pallas kernels for 5%

profile of v3, /device:TPU:1, one launch (start us, length us, event | category | flops | bytes accessed | tf_op | source)
XLA Modules:
  0.0 76.4 jit_solution(9014007545524839725)
XLA Ops:
  0.6 2.2 %shard_map.67 = bf16[64,4,1280]{2,1,0:T(4,128)(2,1)} custom-call(s32[1,128]{1,0:T(1,128)} %bitcast.4, bf16[128,1152]{1,0:T(8,128)(2,1)} %queries_hbm.1), custom_call_target="tpu_custom_call" | custom-call | tf_op jit(solution)/shard_map/pallas_call | solution.py:226
  2.8 13.0 %all-to-all-start = ((bf16[64,4,1280]{2,1,0:T(4,128)(2,1)}), bf16[64,4,1280]{2,1,0:T(4,128)(2,1)S(1)}, u32[]{:S(2)}, u32[]{:S(2)}) async-start(bf16[64,4,1280]{2,1,0:T(4,128)(2,1)} %shard_map.67), calls=%async_computation | async-start | bytes 1310720 | tf_op jit(solution)/shard_map/all_to_all | solution.py:258
  15.8 1.2 %dynamic_slice.3 = s32[1]{0:T(128)} dynamic-slice(s32[64]{0:T(128)} %param.7, s32[]{:T(128)S(6)} %select_n.3), dynamic_slice_sizes={1} | dynamic-slice | bytes 12 | tf_op jit(solution)/shard_map/dynamic_slice | solution.py:239
  17.1 0.0 copy-start
  17.1 2.3 %copy-done = bf16[2048,1152]{1,0:T(8,128)(2,1)S(1)} copy-done((bf16[2048,1152]{1,0:T(8,128)(2,1)S(1)}, bf16[2048,1152]{1,0:T(8,128)(2,1)}, u32[]{:S(2)}) %copy-start) | copy-done | bytes 4718616
  19.4 1.4 %shard_map.68 = (f32[1,2048]{1,0:T(1,128)S(1)}, bf16[1024,1152]{1,0:T(8,128)(2,1)S(1)}, bf16[1024,1152]{1,0:T(8,128)(2,1)S(1)}) custom-call(bf16[2048,1152]{1,0:T(8,128)(2,1)S(1)} %copy-done), custom_call_target="tpu_custom_call" | custom-call | flops 4718592 | bytes 4718592 | tf_op jit(solution)/shard_map/pallas_call | solution.py:245
  20.8 0.0 copy-start.1
  20.8 1.4 %copy-done.1 = bf16[1024,1152]{1,0:T(8,128)(2,1)} copy-done((bf16[1024,1152]{1,0:T(8,128)(2,1)}, bf16[1024,1152]{1,0:T(8,128)(2,1)S(1)}, u32[]{:S(2)}) %copy-start.1) | copy-done | bytes 2359320
  22.2 0.7 pad_add_fusion.info_ref
  22.9 13.2 %all-to-all-done.got_ref = bf16[64,4,1280]{2,1,0:T(4,128)(2,1)S(1)} async-done(((bf16[64,4,1280]{2,1,0:T(4,128)(2,1)}), bf16[64,4,1280]{2,1,0:T(4,128)(2,1)S(1)}, u32[]{:S(2)}, u32[]{:S(2)}) %all-to-all-start) | async-done | bytes 655392 | tf_op jit(solution)/shard_map/all_to_all | solution.py:258
  36.2 0.0 copy-start.2
  36.2 1.5 %shard_map.69 = (f32[256,1024]{1,0:T(8,128)S(1)}, bf16[256,1280]{1,0:T(8,128)(2,1)S(1)}, f32[3,256,128]{2,1,0:T(8,128)S(1)}) custom-call(s32[2]{0:T(128)S(1)} %pad_add_fusion.info_ref, bf16[64,4,1280]{2,1,0:T(4,128)(2,1)S(1)} %all-to-all-done.got_ref, bf16[1024,1152]{1,0:T(8,128)(2,1)S(1)} %get-tuple-element.17.near_ref, ...), custom_call_target="tpu_custom_call" | custom-call | flops 603979776 | bytes 2359296 | tf_op jit(solution)/shard_map/pallas_call | solution.py:261
  37.7 0.1 copy-done.2
  37.8 1.8 %shard_map.70 = (f32[256,1024]{1,0:T(8,128)S(1)}, f32[256,128]{1,0:T(8,128)S(1)}, f32[1,128]{1,0:T(1,128)S(1)}) custom-call(s32[2]{0:T(128)S(1)} %pad_add_fusion.info_ref, bf16[256,1280]{1,0:T(8,128)(2,1)S(1)} %get-tuple-element.20.rows_ref, f32[3,256,128]{2,1,0:T(8,128)S(1)} %get-tuple-element.21.state_ref, bf16[1024,1152]{1,0:T(8,128)(2,1)S(1)} %copy-done.2, ...), custom_call_target="tpu_custom_call" | custom-call | flops 603979776 | bytes 2359296 | tf_op jit(solution)/shard_map/pallas_call | solution.py:273
  39.6 2.8 %collective-permute-start.2 = (f32[1,128]{1,0:T(1,128)S(1)}, f32[1,128]{1,0:T(1,128)S(1)}, u32[]{:S(2)}, u32[]{:S(2)}) collective-permute-start(f32[1,128]{1,0:T(1,128)S(1)} %get-tuple-element.27.refs_0_), channel_id=1, source_target_pairs={{0,3},{1,0},{2,1},{3,2},{4,7},{5,4},{6,5},{7,6},{8,11},{9,8},{10,9... | collective-permute-start | bytes 1544 | tf_op jit(solution)/shard_map/ppermute | solution.py:210
  42.4 0.4 collective-permute-start.1
  42.8 0.7 collective-permute-start
  43.5 2.2 %shard_map.71 = (f32[256,1152]{1,0:T(8,128)S(1)}, f32[256,128]{1,0:T(8,128)S(1)}) custom-call(s32[2]{0:T(128)S(1)} %pad_add_fusion.info_ref, f32[256,1024]{1,0:T(8,128)S(1)} %get-tuple-element.19.cos_near_ref, f32[256,1024]{1,0:T(8,128)S(1)} %get-tuple-element.23.cos_rest_ref, f32[256,128]{1,0:T(8,128)S(1)} %get-tuple-element.24.best_ref, ...), custom_call_target="tpu_custom_call" | custom-call | flops 2415919104 | bytes 18874368 | tf_op jit(solution)/shard_map/pallas_call | solution.py:286
  45.7 0.0 copy-start.3
  45.7 0.0 collective-permute-done.2.refs_3_
  45.8 0.6 collective-permute-done.1.refs_2_
  46.3 0.1 collective-permute-done.refs_1_
  46.4 0.6 shard_map.72
  47.0 27.7 %all_to_all.10.back_ref = s16[64,4,1280]{2,1,0:T(4,128)(2,1)S(1)} all-to-all(s16[64,4,1280]{2,1,0:T(4,128)(2,1)S(1)} %shard_map.72), channel_id=1, replica_groups=mesh['store'=64,'batch'=4] {'store'}, dimensions={0} | all-to-all | bytes 1310720 | tf_op jit(solution)/shard_map/all_to_all | solution.py:305
  74.8 0.0 copy-done.3
  74.8 1.7 %shard_map.73 = (f32[128,1152]{1,0:T(8,128)}, f32[2,128]{1,0:T(2,128)}, f32[1,128]{1,0:T(1,128)}) custom-call(s32[1,128]{1,0:T(1,128)S(1)} %bitcast.5, s16[64,4,1280]{2,1,0:T(4,128)(2,1)S(1)} %all_to_all.10.back_ref), custom_call_target="tpu_custom_call" | custom-call | tf_op jit(solution)/shard_map/pallas_call | solution.py:307
Async XLA Ops:
  2.8 33.4 %all-to-all-start = ((bf16[64,4,1280]{2,1,0:T(4,128)(2,1)}), bf16[64,4,1280]{2,1,0:T(4,128)(2,1)S(1)}, u32[]{:S(2)}, u32[]{:S(2)}) async-start(bf16[64,4,1280]{2,1,0:T(4,128)(2,1)} %shard_map.67), calls=%async_computation | async-start | bytes 1310720 | tf_op jit(solution)/shard_map/all_to_all | solution.py:258
  17.1 2.3 %copy-start = (bf16[2048,1152]{1,0:T(8,128)(2,1)S(1)}, bf16[2048,1152]{1,0:T(8,128)(2,1)}, u32[]{:S(2)}) copy-start(bf16[2048,1152]{1,0:T(8,128)(2,1)} %store_hbm.1) | copy-start | bytes 14155780
  20.8 1.4 %copy-start.1 = (bf16[1024,1152]{1,0:T(8,128)(2,1)}, bf16[1024,1152]{1,0:T(8,128)(2,1)S(1)}, u32[]{:S(2)}) copy-start(bf16[1024,1152]{1,0:T(8,128)(2,1)S(1)} %get-tuple-element.22.rest_ref) | copy-start | bytes 7077892
  36.2 1.7 %copy-start.2 = (bf16[1024,1152]{1,0:T(8,128)(2,1)S(1)}, bf16[1024,1152]{1,0:T(8,128)(2,1)}, u32[]{:S(2)}) copy-start(bf16[1024,1152]{1,0:T(8,128)(2,1)} %copy-done.1) | copy-start | bytes 7077892
  39.6 6.1 %collective-permute-start.2 = (f32[1,128]{1,0:T(1,128)S(1)}, f32[1,128]{1,0:T(1,128)S(1)}, u32[]{:S(2)}, u32[]{:S(2)}) collective-permute-start(f32[1,128]{1,0:T(1,128)S(1)} %get-tuple-element.27.refs_0_), channel_id=1, source_target_pairs={{0,3},{1,0},{2,1},{3,2},{4,7},{5,4},{6,5},{7,6},{8,11},{9,8},{10,9... | collective-permute-start | bytes 1544 | tf_op jit(solution)/shard_map/ppermute | solution.py:210
  42.4 3.9 %collective-permute-start.1 = (f32[1,128]{1,0:T(1,128)S(1)}, f32[1,128]{1,0:T(1,128)S(1)}, u32[]{:S(2)}, u32[]{:S(2)}) collective-permute-start(f32[1,128]{1,0:T(1,128)S(1)} %get-tuple-element.27.refs_0_), channel_id=1, source_target_pairs={{0,2},{1,3},{2,0},{3,1},{4,6},{5,7},{6,4},{7,5},{8,10},{9,11},{10,... | collective-permute-start | bytes 1544 | tf_op jit(solution)/shard_map/ppermute | solution.py:210
  42.8 3.6 %collective-permute-start = (f32[1,128]{1,0:T(1,128)S(1)}, f32[1,128]{1,0:T(1,128)S(1)}, u32[]{:S(2)}, u32[]{:S(2)}) collective-permute-start(f32[1,128]{1,0:T(1,128)S(1)} %get-tuple-element.27.refs_0_), channel_id=1, source_target_pairs={{0,1},{1,2},{2,3},{3,0},{4,5},{5,6},{6,7},{7,4},{8,9},{9,10},{10,1... | collective-permute-start | bytes 1544 | tf_op jit(solution)/shard_map/ppermute | solution.py:210
  45.7 29.0 %copy-start.3 = (s32[128]{0:T(128)S(1)}, s32[128]{0:T(128)}, u32[]{:S(2)}) copy-start(s32[128]{0:T(128)} %param.5) | copy-start | bytes 1540

commit v4 on v3

--- a/solution.py
+++ b/solution.py
@@ -11,6 +11,7 @@
 normalized_sharpness = 160.0
 epsilon = 1e-06
 EXTRA = 128
+SIDE = 2
 STEPS = 32767.0
 COSINE_UNIT = 16384.0
 NOVELTY_UNIT = 8192.0
@@ -24,6 +25,14 @@
     return lax.dot_general(a, b, ((contract[:1], contract[1:]), ((), ())), preferred_element_type=jnp.float32)
 
 
+def slot_of(cluster, rank, clusters):
+    return rank // 2 * (2 * clusters) + cluster * 2 + rank % 2
+
+
+def shifted(value, count):
+    return jnp.concatenate([value[:, -count:], value[:, :-count]], axis=1) if count else value
+
+
 def cluster_pairs(cluster_ref):
     across = jnp.broadcast_to(cluster_ref[...], (cluster_ref.shape[1],) * 2)
     down = across.T
@@ -32,7 +41,7 @@
     return across, down, i, j
 
 
-def place_kernel(depth, cluster_hbm, queries_hbm, out_ref, cluster_ref, queries_ref, cluster_sem, queries_sem):
+def place_kernel(cluster_hbm, queries_hbm, out_ref, cluster_ref, queries_ref, cluster_sem, queries_sem):
     copy_cluster = pltpu.make_async_copy(cluster_hbm, cluster_ref, cluster_sem)
     copy_queries = pltpu.make_async_copy(queries_hbm, queries_ref, queries_sem)
     copy_cluster.start()
@@ -40,17 +49,22 @@
     copy_cluster.wait()
     across, down, i, j = cluster_pairs(cluster_ref)
     rows, features = queries_ref.shape
+    clusters, pair, _ = out_ref.shape
     rank = jnp.sum(jnp.where((across == down) & (i < j), 1.0, 0.0), axis=0, keepdims=True)
-    slot = across[:1] * depth + rank.astype(jnp.int32)
-    slots = out_ref.shape[0] * depth
-    place = jnp.where(lax.broadcasted_iota(jnp.int32, (slots, rows), 0) == slot, 1.0, 0.0)
+    slot = slot_of(across[:1], rank.astype(jnp.int32), clusters)
+    step = clusters * pair
+    place = jnp.where(lax.broadcasted_iota(jnp.int32, (SIDE * step, rows), 0) == slot, 1.0, 0.0)
     place = place.astype(jnp.bfloat16)
-    tail = jnp.where(j == 0, i.astype(jnp.float32), jnp.where(j == 1, 1.0, 0.0))
-    sent = dot(place, tail.astype(jnp.bfloat16), (1, 0)).astype(jnp.bfloat16)
-    out_ref[:, :, features:] = sent.reshape(-1, depth, EXTRA)
+    extra = jnp.zeros((step, EXTRA), jnp.float32)
+    for h in range(SIDE):
+        at = h * (EXTRA // SIDE)
+        tail = jnp.where(j == at, i.astype(jnp.float32), jnp.where(j == at + 1, 1.0, 0.0))
+        extra = extra + dot(place[h * step : (h + 1) * step], tail.astype(jnp.bfloat16), (1, 0))
+    out_ref[:, :, SIDE * features :] = extra.astype(jnp.bfloat16).reshape(clusters, pair, EXTRA)
     copy_queries.wait()
-    sent = dot(place, queries_ref[...], (1, 0)).astype(jnp.bfloat16)
-    out_ref[:, :, :features] = sent.reshape(-1, depth, features)
+    for h in range(SIDE):
+        sent = dot(place[h * step : (h + 1) * step], queries_ref[...], (1, 0)).astype(jnp.bfloat16)
+        out_ref[:, :, h * features : (h + 1) * features] = sent.reshape(clusters, pair, features)
 
 
 def scale_kernel(store_hbm, scale_ref, near_ref, rest_ref, near_sem, rest_sem):
@@ -93,9 +107,15 @@
 
 
 def near_kernel(info_ref, got_ref, near_ref, scale_ref, cos_ref, rows_ref, state_ref):
-    sources, depth, width = got_ref.shape
-    slots, features = sources * depth, width - EXTRA
-    rows_ref[...] = got_ref[...].reshape(slots, width)
+    sources, pair, width = got_ref.shape
+    features = (width - EXTRA) // SIDE
+    step = sources * pair
+    slots = SIDE * step
+    extra = got_ref[:, :, SIDE * features :].reshape(step, EXTRA).astype(jnp.float32)
+    for h in range(SIDE):
+        span = slice(h * step, (h + 1) * step)
+        rows_ref[span, :features] = got_ref[:, :, h * features : (h + 1) * features].reshape(step, features)
+        rows_ref[span, features:] = shifted(extra, h * (EXTRA // SIDE)).astype(rows_ref.dtype)
     rows = rows_ref[:, :features]
     wide = rows.astype(jnp.float32)
     row_scale = lax.rsqrt(jnp.sum(wide * wide, axis=1, keepdims=True) + epsilon)
@@ -105,14 +125,14 @@
 
 
 def rest_kernel(
-    growth, n_batch, rows_dev, depth, info_ref, rows_ref, state_ref, rest_ref, scale_ref, cos_ref, best_ref, sums_ref
+    growth, n_batch, rows_dev, n_store, info_ref, rows_ref, state_ref, rest_ref, scale_ref, cos_ref, best_ref, sums_ref
 ):
     slots, width = rows_ref.shape
     features = width - EXTRA
     live, batch = info_ref[0], info_ref[1]
     tail = rows_ref[:, features:].astype(jnp.float32)
     slot = lax.broadcasted_iota(jnp.int32, (slots, 1), 0)
-    index = (slot // depth * n_batch + batch) * rows_dev + tail[:, :1].astype(jnp.int32)
+    index = (slot % (2 * n_store) // 2 * n_batch + batch) * rows_dev + tail[:, :1].astype(jnp.int32)
     recency = jnp.exp(index.astype(jnp.float32) * growth) * tail[:, 1:2]
     base = scale_ref.shape[1] - rest_ref.shape[0]
     one, two = cosines(
@@ -150,9 +170,10 @@
 
 def code_kernel(weighted_ref, total_ref, best_ref, *refs):
     *sums_refs, out_ref = refs
-    sources, depth, width = out_ref.shape
-    features = width - EXTRA
-    slots = sources * depth
+    sources, pair, width = out_ref.shape
+    features = (width - EXTRA) // SIDE
+    step = sources * pair
+    slots = SIDE * step
     sums = sums_refs[0][...]
     for ref in sums_refs[1:]:
         sums = sums + ref[...]
@@ -161,19 +182,23 @@
     total = jnp.sum(total_ref[...], axis=1, keepdims=True)
     weighted = weighted_ref[...]
     largest = jnp.maximum(jnp.max(jnp.abs(weighted), axis=1, keepdims=True), 1e-30)
-    coded = jnp.round(weighted * (STEPS / largest)).astype(jnp.int32)
-    out_ref[:, :, :features] = coded.reshape(sources, depth, features).astype(jnp.int16)
+    coded = jnp.round(weighted * (STEPS / largest)).astype(jnp.int32).astype(jnp.int16)
+    for h in range(SIDE):
+        part = coded[h * step : (h + 1) * step].reshape(sources, pair, features)
+        out_ref[:, :, h * features : (h + 1) * features] = part
     values = (
         parts(first, COSINE_UNIT)
         + parts(second, COSINE_UNIT)
         + parts(jnp.log(largest / total), LOG_UNIT)
         + parts(first - mean, NOVELTY_UNIT)
     )
-    lane = lax.broadcasted_iota(jnp.int32, (slots, 128), 1)
-    extra = jnp.zeros((slots, 128), jnp.float32)
+    lane = lax.broadcasted_iota(jnp.int32, (step, EXTRA), 1)
+    extra = jnp.zeros((step, EXTRA), jnp.float32)
     for k, value in enumerate(values):
-        extra = jnp.where(lane == k, value, extra)
-    out_ref[:, :, features:] = extra.astype(jnp.int32).reshape(sources, depth, EXTRA).astype(jnp.int16)
+        for h in range(SIDE):
+            extra = jnp.where(lane == k + h * (EXTRA // SIDE), value[h * step : (h + 1) * step], extra)
+    extra = extra.astype(jnp.int32).astype(jnp.int16)
+    out_ref[:, :, SIDE * features :] = extra.reshape(sources, pair, EXTRA)
 
 
 def joined(high, low, unit):
@@ -182,23 +207,26 @@
 
 def pick_kernel(cluster_ref, back_ref, near_ref, best_ref, novelty_ref):
     across, down, i, j = cluster_pairs(cluster_ref)
-    clusters, depth, width = back_ref.shape
-    features = width - EXTRA
-    slots = clusters * depth
+    clusters, pair, width = back_ref.shape
+    features = (width - EXTRA) // SIDE
+    step = clusters * pair
     rank = jnp.sum(jnp.where((across == down) & (j < i), 1.0, 0.0), axis=1, keepdims=True)
-    slot = down[:, :1] * depth + rank.astype(jnp.int32)
-    pick = jnp.where(lax.broadcasted_iota(jnp.int32, (i.shape[0], slots), 1) == slot, 1.0, 0.0)
+    slot = slot_of(down[:, :1], rank.astype(jnp.int32), clusters)
+    pick = jnp.where(lax.broadcasted_iota(jnp.int32, (i.shape[0], SIDE * step), 1) == slot, 1.0, 0.0)
     pick = pick.astype(jnp.bfloat16)
 
-    def mine(value):
-        value = value.astype(jnp.float32).reshape(slots, -1)
-        high = jnp.floor(value * (1.0 / 256.0))
-        low = value - high * 256.0
-        return dot(pick, high.astype(jnp.bfloat16), (1, 0)) * 256.0 + dot(pick, low.astype(jnp.bfloat16), (1, 0))
-
-    extra = mine(back_ref[:, :, features:])
+    pick = jnp.concatenate([pick, pick], axis=1)
+
+    def mine(halves):
+        value = jnp.concatenate(halves, axis=0).astype(jnp.float32)
+        high = jnp.floor(value * (1.0 / 256.0)) * 256.0
+        return dot(pick, jnp.concatenate([high, value - high], axis=0).astype(jnp.bfloat16), (1, 0))
+
+    extra = back_ref[:, :, SIDE * features :].reshape(step, EXTRA).astype(jnp.float32)
+    extra = mine([shifted(extra, h * (EXTRA // SIDE)) for h in range(SIDE)])
     largest = jnp.exp(joined(extra[:, 4:5], extra[:, 5:6], LOG_UNIT))
-    near_ref[...] = mine(back_ref[:, :, :features]) * (largest * (1.0 / STEPS))
+    rows = mine([back_ref[:, :, h * features : (h + 1) * features].reshape(step, features) for h in range(SIDE)])
+    near_ref[...] = rows * (largest * (1.0 / STEPS))
     extra = extra.T
     best_ref[0:1, :] = joined(extra[0:1], extra[1:2], COSINE_UNIT)
     best_ref[1:2, :] = joined(extra[2:3], extra[3:4], COSINE_UNIT)
@@ -218,14 +246,16 @@
     crows = store.shape[0]
     depth = 2 * rows_dev // clusters
     slots = clusters * depth
+    pair = depth // SIDE
     width = features + EXTRA
+    wide = SIDE * features + EXTRA
     growth = math.log(3.0) / (rows_dev * n_store * n_batch)
     params = pltpu.CompilerParams(vmem_limit_bytes=VMEM_BYTES)
 
     cluster_row = query_cluster.reshape(1, rows_dev)
     send = pl.pallas_call(
-        functools.partial(place_kernel, depth),
-        out_shape=jax.ShapeDtypeStruct((clusters, depth, width), jnp.bfloat16),
+        place_kernel,
+        out_shape=jax.ShapeDtypeStruct((clusters, pair, wide), jnp.bfloat16),
         in_specs=[pl.BlockSpec(memory_space=pltpu.HBM)] * 2,
         scratch_shapes=[
             pltpu.VMEM((1, rows_dev), jnp.int32),
@@ -271,7 +301,7 @@
         cost_estimate=half_cost,
     )(info, got, store_near, store_scale)
     cos_rest, best, sums = pl.pallas_call(
-        functools.partial(rest_kernel, growth, n_batch, rows_dev, depth),
+        functools.partial(rest_kernel, growth, n_batch, rows_dev, n_store),
         out_shape=(
             jax.ShapeDtypeStruct((slots, crows - near), f32),
             jax.ShapeDtypeStruct((slots, 128), f32),
@@ -297,7 +327,7 @@
     )(info, cos_near, cos_rest, best, store_near, store_rest)
     back = pl.pallas_call(
         code_kernel,
-        out_shape=jax.ShapeDtypeStruct((n_store, depth, width), jnp.int16),
+        out_shape=jax.ShapeDtypeStruct((n_store, pair, wide), jnp.int16),
         in_specs=[vmem] * (3 + n_batch),
         out_specs=vmem,
         compiler_params=params,

time: 76.7 us -> 75.4 us (0.983)
  no operation moved by 1% of the time
where the time goes in v4:
time: 75.4 us; the launch traced here: 75.1 us
  blocking collectives  27 us (36%)
  starting transfers between devices  16.9 us (22%)
  waiting for transfers between devices  13.2 us (18%)
  Pallas kernels  11.4 us (15%)
  local copies, waits for them, and re-layouts  5.13 us (7%)
    all_to_all x1, blocking collectives, body(): lax.all_to_all(back, 'store', split_axis=0, concat_axis=0, tiled=True)  27 us
    all_to_all x1, starting transfers between devices, body(): got = lax.all_to_all(send, 'store', split_axis=0, concat_axis=0, tiled=True)  13 us
    all_to_all x1, waiting for transfers between devices, body(): got = lax.all_to_all(send, 'store', split_axis=0, concat_axis=0, tiled=True)  12.6 us
    unnamed x8, local copies, waits for them, and re-layouts  3.88 us
    ppermute x3, starting transfers between devices, over_batch(): lax.ppermute(value, 'batch', [(i, (i + k) % n) for i in range(n)])  3.85 us
    pallas_call x1, Pallas kernels, body(): pl.pallas_call(weigh_kernel, out_shape=(jax.ShapeDtypeStruct((slots, feat...  2.25 us
    pallas_call x1, Pallas kernels, body(): pl.pallas_call(place_kernel, out_shape=jax.ShapeDtypeStruct((clusters, pa...  2.16 us
    pallas_call x1, Pallas kernels, body(): pl.pallas_call(functools.partial(rest_kernel, growth, n_batch, rows_dev,...  1.79 us
  transfers between devices with their start and end apart: 4, of which 3 were waited for; matrix products, arithmetic and copies ran while one was open for 3% of the time, Pallas kernels for 5%

profile of v4, /device:TPU:1, one launch (start us, length us, event | category | flops | bytes accessed | tf_op | source)
XLA Modules:
  0.0 75.1 jit_solution(5027556583949837101)
XLA Ops:
  0.6 2.2 %shard_map.67 = bf16[64,2,2432]{2,1,0:T(2,128)(2,1)} custom-call(s32[1,128]{1,0:T(1,128)} %bitcast.4, bf16[128,1152]{1,0:T(8,128)(2,1)} %queries_hbm.1), custom_call_target="tpu_custom_call" | custom-call | tf_op jit(solution)/shard_map/pallas_call | solution.py:256
  2.8 13.0 %all-to-all-start = ((bf16[64,2,2432]{2,1,0:T(2,128)(2,1)}), bf16[64,2,2432]{2,1,0:T(2,128)(2,1)S(1)}, u32[]{:S(2)}, u32[]{:S(2)}) async-start(bf16[64,2,2432]{2,1,0:T(2,128)(2,1)} %shard_map.67), calls=%async_computation | async-start | bytes 1245184 | tf_op jit(solution)/shard_map/all_to_all | solution.py:288
  15.8 1.2 %dynamic_slice.3 = s32[1]{0:T(128)} dynamic-slice(s32[64]{0:T(128)} %param.7, s32[]{:T(128)S(6)} %select_n.3), dynamic_slice_sizes={1} | dynamic-slice | bytes 12 | tf_op jit(solution)/shard_map/dynamic_slice | solution.py:269
  17.1 0.0 copy-start
  17.1 2.3 %copy-done = bf16[2048,1152]{1,0:T(8,128)(2,1)S(1)} copy-done((bf16[2048,1152]{1,0:T(8,128)(2,1)S(1)}, bf16[2048,1152]{1,0:T(8,128)(2,1)}, u32[]{:S(2)}) %copy-start) | copy-done | bytes 4718616
  19.4 1.4 %shard_map.68 = (f32[1,2048]{1,0:T(1,128)S(1)}, bf16[1024,1152]{1,0:T(8,128)(2,1)S(1)}, bf16[1024,1152]{1,0:T(8,128)(2,1)S(1)}) custom-call(bf16[2048,1152]{1,0:T(8,128)(2,1)S(1)} %copy-done), custom_call_target="tpu_custom_call" | custom-call | flops 4718592 | bytes 4718592 | tf_op jit(solution)/shard_map/pallas_call | solution.py:275
  20.8 0.0 copy-start.1
  20.8 1.4 %copy-done.1 = bf16[1024,1152]{1,0:T(8,128)(2,1)} copy-done((bf16[1024,1152]{1,0:T(8,128)(2,1)}, bf16[1024,1152]{1,0:T(8,128)(2,1)S(1)}, u32[]{:S(2)}) %copy-start.1) | copy-done | bytes 2359320
  22.2 0.7 pad_add_fusion.info_ref
  22.9 12.6 %all-to-all-done.got_ref = bf16[64,2,2432]{2,1,0:T(2,128)(2,1)S(1)} async-done(((bf16[64,2,2432]{2,1,0:T(2,128)(2,1)}), bf16[64,2,2432]{2,1,0:T(2,128)(2,1)S(1)}, u32[]{:S(2)}, u32[]{:S(2)}) %all-to-all-start) | async-done | bytes 622624 | tf_op jit(solution)/shard_map/all_to_all | solution.py:288
  35.5 0.0 copy-start.2
  35.5 1.5 %shard_map.69 = (f32[256,1024]{1,0:T(8,128)S(1)}, bf16[256,1280]{1,0:T(8,128)(2,1)S(1)}, f32[3,256,128]{2,1,0:T(8,128)S(1)}) custom-call(s32[2]{0:T(128)S(1)} %pad_add_fusion.info_ref, bf16[64,2,2432]{2,1,0:T(2,128)(2,1)S(1)} %all-to-all-done.got_ref, bf16[1024,1152]{1,0:T(8,128)(2,1)S(1)} %get-tuple-element.17.near_ref, ...), custom_call_target="tpu_custom_call" | custom-call | flops 603979776 | bytes 2359296 | tf_op jit(solution)/shard_map/pallas_call | solution.py:291
  37.1 0.1 copy-done.2
  37.2 1.8 %shard_map.70 = (f32[256,1024]{1,0:T(8,128)S(1)}, f32[256,128]{1,0:T(8,128)S(1)}, f32[1,128]{1,0:T(1,128)S(1)}) custom-call(s32[2]{0:T(128)S(1)} %pad_add_fusion.info_ref, bf16[256,1280]{1,0:T(8,128)(2,1)S(1)} %get-tuple-element.20.rows_ref, f32[3,256,128]{2,1,0:T(8,128)S(1)} %get-tuple-element.21.state_ref, bf16[1024,1152]{1,0:T(8,128)(2,1)S(1)} %copy-done.2, ...), custom_call_target="tpu_custom_call" | custom-call | flops 603979776 | bytes 2359296 | tf_op jit(solution)/shard_map/pallas_call | solution.py:303
  39.0 2.8 %collective-permute-start.2 = (f32[1,128]{1,0:T(1,128)S(1)}, f32[1,128]{1,0:T(1,128)S(1)}, u32[]{:S(2)}, u32[]{:S(2)}) collective-permute-start(f32[1,128]{1,0:T(1,128)S(1)} %get-tuple-element.27.refs_0_), channel_id=1, source_target_pairs={{0,3},{1,0},{2,1},{3,2},{4,7},{5,4},{6,5},{7,6},{8,11},{9,8},{10,9... | collective-permute-start | bytes 1544 | tf_op jit(solution)/shard_map/ppermute | solution.py:238
  41.8 0.3 collective-permute-start.1
  42.1 0.7 collective-permute-start
  42.8 2.2 %shard_map.71 = (f32[256,1152]{1,0:T(8,128)S(1)}, f32[256,128]{1,0:T(8,128)S(1)}) custom-call(s32[2]{0:T(128)S(1)} %pad_add_fusion.info_ref, f32[256,1024]{1,0:T(8,128)S(1)} %get-tuple-element.19.cos_near_ref, f32[256,1024]{1,0:T(8,128)S(1)} %get-tuple-element.23.cos_rest_ref, f32[256,128]{1,0:T(8,128)S(1)} %get-tuple-element.24.best_ref, ...), custom_call_target="tpu_custom_call" | custom-call | flops 2415919104 | bytes 18874368 | tf_op jit(solution)/shard_map/pallas_call | solution.py:316
  45.1 0.0 copy-start.3
  45.1 0.0 collective-permute-done.2.refs_3_
  45.1 0.6 collective-permute-done.1.refs_2_
  45.7 0.1 collective-permute-done.refs_1_
  45.7 0.6 shard_map.72
  46.4 27.0 %all_to_all.10.back_ref = s16[64,2,2432]{2,1,0:T(2,128)(2,1)S(1)} all-to-all(s16[64,2,2432]{2,1,0:T(2,128)(2,1)S(1)} %shard_map.72), channel_id=1, replica_groups=mesh['store'=64,'batch'=4] {'store'}, dimensions={0} | all-to-all | bytes 1245184 | tf_op jit(solution)/shard_map/all_to_all | solution.py:335
  73.4 0.0 copy-done.3
  73.4 1.7 %shard_map.73 = (f32[128,1152]{1,0:T(8,128)}, f32[2,128]{1,0:T(2,128)}, f32[1,128]{1,0:T(1,128)}) custom-call(s32[1,128]{1,0:T(1,128)S(1)} %bitcast.5, s16[64,2,2432]{2,1,0:T(2,128)(2,1)S(1)} %all_to_all.10.back_ref), custom_call_target="tpu_custom_call" | custom-call | tf_op jit(solution)/shard_map/pallas_call | solution.py:337
Async XLA Ops:
  2.8 32.7 %all-to-all-start = ((bf16[64,2,2432]{2,1,0:T(2,128)(2,1)}), bf16[64,2,2432]{2,1,0:T(2,128)(2,1)S(1)}, u32[]{:S(2)}, u32[]{:S(2)}) async-start(bf16[64,2,2432]{2,1,0:T(2,128)(2,1)} %shard_map.67), calls=%async_computation | async-start | bytes 1245184 | tf_op jit(solution)/shard_map/all_to_all | solution.py:288
  17.1 2.3 %copy-start = (bf16[2048,1152]{1,0:T(8,128)(2,1)S(1)}, bf16[2048,1152]{1,0:T(8,128)(2,1)}, u32[]{:S(2)}) copy-start(bf16[2048,1152]{1,0:T(8,128)(2,1)} %store_hbm.1) | copy-start | bytes 14155780
  20.8 1.4 %copy-start.1 = (bf16[1024,1152]{1,0:T(8,128)(2,1)}, bf16[1024,1152]{1,0:T(8,128)(2,1)S(1)}, u32[]{:S(2)}) copy-start(bf16[1024,1152]{1,0:T(8,128)(2,1)S(1)} %get-tuple-element.22.rest_ref) | copy-start | bytes 7077892
  35.5 1.7 %copy-start.2 = (bf16[1024,1152]{1,0:T(8,128)(2,1)S(1)}, bf16[1024,1152]{1,0:T(8,128)(2,1)}, u32[]{:S(2)}) copy-start(bf16[1024,1152]{1,0:T(8,128)(2,1)} %copy-done.1) | copy-start | bytes 7077892
  39.0 6.1 %collective-permute-start.2 = (f32[1,128]{1,0:T(1,128)S(1)}, f32[1,128]{1,0:T(1,128)S(1)}, u32[]{:S(2)}, u32[]{:S(2)}) collective-permute-start(f32[1,128]{1,0:T(1,128)S(1)} %get-tuple-element.27.refs_0_), channel_id=1, source_target_pairs={{0,3},{1,0},{2,1},{3,2},{4,7},{5,4},{6,5},{7,6},{8,11},{9,8},{10,9... | collective-permute-start | bytes 1544 | tf_op jit(solution)/shard_map/ppermute | solution.py:238
  41.8 3.9 %collective-permute-start.1 = (f32[1,128]{1,0:T(1,128)S(1)}, f32[1,128]{1,0:T(1,128)S(1)}, u32[]{:S(2)}, u32[]{:S(2)}) collective-permute-start(f32[1,128]{1,0:T(1,128)S(1)} %get-tuple-element.27.refs_0_), channel_id=1, source_target_pairs={{0,2},{1,3},{2,0},{3,1},{4,6},{5,7},{6,4},{7,5},{8,10},{9,11},{10,... | collective-permute-start | bytes 1544 | tf_op jit(solution)/shard_map/ppermute | solution.py:238
  42.1 3.6 %collective-permute-start = (f32[1,128]{1,0:T(1,128)S(1)}, f32[1,128]{1,0:T(1,128)S(1)}, u32[]{:S(2)}, u32[]{:S(2)}) collective-permute-start(f32[1,128]{1,0:T(1,128)S(1)} %get-tuple-element.27.refs_0_), channel_id=1, source_target_pairs={{0,1},{1,2},{2,3},{3,0},{4,5},{5,6},{6,7},{7,4},{8,9},{9,10},{10,1... | collective-permute-start | bytes 1544 | tf_op jit(solution)/shard_map/ppermute | solution.py:238
  45.1 28.3 %copy-start.3 = (s32[128]{0:T(128)S(1)}, s32[128]{0:T(128)}, u32[]{:S(2)}) copy-start(s32[128]{0:T(128)} %param.5) | copy-start | bytes 1540

commit v5 on v4

--- a/solution.py
+++ b/solution.py
@@ -235,7 +235,8 @@
 
 def over_batch(value):
     n = lax.axis_size("batch")
-    return [value] + [lax.ppermute(value, "batch", [(i, (i + k) % n) for i in range(n)]) for k in range(1, n)]
+    shifts = sorted(range(1, n), key=lambda k: -min(k, n - k))
+    return [value] + [lax.ppermute(value, "batch", [(i, (i + k) % n) for i in range(n)]) for k in shifts]
 
 
 def body(queries, query_cluster, store, store_counts):

time: 75.4 us -> 75.1 us (level)
  transfers between devices with their start and end apart: 4 -> 4, of which waited for: 3 -> 1; matrix products, arithmetic and copies ran while one was open for 3% -> 3% of each run, Pallas kernels for 5% -> 5%
where the time goes in v5:
time: 75.1 us; the launch traced here: 74.7 us
  blocking collectives  26.7 us (36%)
  starting transfers between devices  17.5 us (23%)
  waiting for transfers between devices  12.6 us (17%)
  Pallas kernels  11.4 us (15%)
  local copies, waits for them, and re-layouts  5.13 us (7%)
    all_to_all x1, blocking collectives, body(): lax.all_to_all(back, 'store', split_axis=0, concat_axis=0, tiled=True)  26.7 us
    all_to_all x1, starting transfers between devices, body(): got = lax.all_to_all(send, 'store', split_axis=0, concat_axis=0, tiled=True)  13 us
    all_to_all x1, waiting for transfers between devices, body(): got = lax.all_to_all(send, 'store', split_axis=0, concat_axis=0, tiled=True)  12.6 us
    ppermute x3, starting transfers between devices, over_batch(): lax.ppermute(value, 'batch', [(i, (i + k) % n) for i in range(n)])  4.46 us
    unnamed x8, local copies, waits for them, and re-layouts  3.88 us
    pallas_call x1, Pallas kernels, body(): pl.pallas_call(weigh_kernel, out_shape=(jax.ShapeDtypeStruct((slots, feat...  2.25 us
    pallas_call x1, Pallas kernels, body(): pl.pallas_call(place_kernel, out_shape=jax.ShapeDtypeStruct((clusters, pa...  2.16 us
    pallas_call x1, Pallas kernels, body(): pl.pallas_call(functools.partial(rest_kernel, growth, n_batch, rows_dev,...  1.79 us
  transfers between devices with their start and end apart: 4, of which 1 were waited for; matrix products, arithmetic and copies ran while one was open for 3% of the time, Pallas kernels for 5%

profile of v5, /device:TPU:1, one launch (start us, length us, event | category | flops | bytes accessed | tf_op | source)
XLA Modules:
  0.0 74.7 jit_solution(8803685906419080539)
XLA Ops:
  0.6 2.2 %shard_map.67 = bf16[64,2,2432]{2,1,0:T(2,128)(2,1)} custom-call(s32[1,128]{1,0:T(1,128)} %bitcast.4, bf16[128,1152]{1,0:T(8,128)(2,1)} %queries_hbm.1), custom_call_target="tpu_custom_call" | custom-call | tf_op jit(solution)/shard_map/pallas_call | solution.py:257
  2.8 13.0 %all-to-all-start = ((bf16[64,2,2432]{2,1,0:T(2,128)(2,1)}), bf16[64,2,2432]{2,1,0:T(2,128)(2,1)S(1)}, u32[]{:S(2)}, u32[]{:S(2)}) async-start(bf16[64,2,2432]{2,1,0:T(2,128)(2,1)} %shard_map.67), calls=%async_computation | async-start | bytes 1245184 | tf_op jit(solution)/shard_map/all_to_all | solution.py:289
  15.8 1.2 %dynamic_slice.3 = s32[1]{0:T(128)} dynamic-slice(s32[64]{0:T(128)} %param.7, s32[]{:T(128)S(6)} %select_n.3), dynamic_slice_sizes={1} | dynamic-slice | bytes 12 | tf_op jit(solution)/shard_map/dynamic_slice | solution.py:270
  17.1 0.0 copy-start
  17.1 2.3 %copy-done = bf16[2048,1152]{1,0:T(8,128)(2,1)S(1)} copy-done((bf16[2048,1152]{1,0:T(8,128)(2,1)S(1)}, bf16[2048,1152]{1,0:T(8,128)(2,1)}, u32[]{:S(2)}) %copy-start) | copy-done | bytes 4718616
  19.4 1.4 %shard_map.68 = (f32[1,2048]{1,0:T(1,128)S(1)}, bf16[1024,1152]{1,0:T(8,128)(2,1)S(1)}, bf16[1024,1152]{1,0:T(8,128)(2,1)S(1)}) custom-call(bf16[2048,1152]{1,0:T(8,128)(2,1)S(1)} %copy-done), custom_call_target="tpu_custom_call" | custom-call | flops 4718592 | bytes 4718592 | tf_op jit(solution)/shard_map/pallas_call | solution.py:276
  20.8 0.0 copy-start.1
  20.8 1.4 %copy-done.1 = bf16[1024,1152]{1,0:T(8,128)(2,1)} copy-done((bf16[1024,1152]{1,0:T(8,128)(2,1)}, bf16[1024,1152]{1,0:T(8,128)(2,1)S(1)}, u32[]{:S(2)}) %copy-start.1) | copy-done | bytes 2359320
  22.2 0.7 pad_add_fusion.info_ref
  22.9 12.6 %all-to-all-done.got_ref = bf16[64,2,2432]{2,1,0:T(2,128)(2,1)S(1)} async-done(((bf16[64,2,2432]{2,1,0:T(2,128)(2,1)}), bf16[64,2,2432]{2,1,0:T(2,128)(2,1)S(1)}, u32[]{:S(2)}, u32[]{:S(2)}) %all-to-all-start) | async-done | bytes 622624 | tf_op jit(solution)/shard_map/all_to_all | solution.py:289
  35.5 0.0 copy-start.2
  35.5 1.5 %shard_map.69 = (f32[256,1024]{1,0:T(8,128)S(1)}, bf16[256,1280]{1,0:T(8,128)(2,1)S(1)}, f32[3,256,128]{2,1,0:T(8,128)S(1)}) custom-call(s32[2]{0:T(128)S(1)} %pad_add_fusion.info_ref, bf16[64,2,2432]{2,1,0:T(2,128)(2,1)S(1)} %all-to-all-done.got_ref, bf16[1024,1152]{1,0:T(8,128)(2,1)S(1)} %get-tuple-element.17.near_ref, ...), custom_call_target="tpu_custom_call" | custom-call | flops 603979776 | bytes 2359296 | tf_op jit(solution)/shard_map/pallas_call | solution.py:292
  37.1 0.1 copy-done.2
  37.2 1.8 %shard_map.70 = (f32[256,1024]{1,0:T(8,128)S(1)}, f32[256,128]{1,0:T(8,128)S(1)}, f32[1,128]{1,0:T(1,128)S(1)}) custom-call(s32[2]{0:T(128)S(1)} %pad_add_fusion.info_ref, bf16[256,1280]{1,0:T(8,128)(2,1)S(1)} %get-tuple-element.20.rows_ref, f32[3,256,128]{2,1,0:T(8,128)S(1)} %get-tuple-element.21.state_ref, bf16[1024,1152]{1,0:T(8,128)(2,1)S(1)} %copy-done.2, ...), custom_call_target="tpu_custom_call" | custom-call | flops 603979776 | bytes 2359296 | tf_op jit(solution)/shard_map/pallas_call | solution.py:304
  39.0 2.8 %collective-permute-start.2 = (f32[1,128]{1,0:T(1,128)S(1)}, f32[1,128]{1,0:T(1,128)S(1)}, u32[]{:S(2)}, u32[]{:S(2)}) collective-permute-start(f32[1,128]{1,0:T(1,128)S(1)} %get-tuple-element.27.refs_0_), channel_id=1, source_target_pairs={{0,3},{1,0},{2,1},{3,2},{4,7},{5,4},{6,5},{7,6},{8,11},{9,8},{10,9... | collective-permute-start | bytes 1544 | tf_op jit(solution)/shard_map/ppermute | solution.py:239
  41.8 0.0 collective-permute-start.1
  41.8 1.6 %collective-permute-start = (f32[1,128]{1,0:T(1,128)S(1)}, f32[1,128]{1,0:T(1,128)S(1)}, u32[]{:S(2)}, u32[]{:S(2)}) collective-permute-start(f32[1,128]{1,0:T(1,128)S(1)} %get-tuple-element.27.refs_0_), channel_id=1, source_target_pairs={{0,2},{1,3},{2,0},{3,1},{4,6},{5,7},{6,4},{7,5},{8,10},{9,11},{10,... | collective-permute-start | bytes 1544 | tf_op jit(solution)/shard_map/ppermute | solution.py:239
  43.4 2.2 %shard_map.71 = (f32[256,1152]{1,0:T(8,128)S(1)}, f32[256,128]{1,0:T(8,128)S(1)}) custom-call(s32[2]{0:T(128)S(1)} %pad_add_fusion.info_ref, f32[256,1024]{1,0:T(8,128)S(1)} %get-tuple-element.19.cos_near_ref, f32[256,1024]{1,0:T(8,128)S(1)} %get-tuple-element.23.cos_rest_ref, f32[256,128]{1,0:T(8,128)S(1)} %get-tuple-element.24.best_ref, ...), custom_call_target="tpu_custom_call" | custom-call | flops 2415919104 | bytes 18874368 | tf_op jit(solution)/shard_map/pallas_call | solution.py:317
  45.7 0.0 copy-start.3
  45.7 0.0 collective-permute-done.2.refs_3_
  45.7 0.0 collective-permute-done.1.refs_2_
  45.7 0.0 collective-permute-done.refs_1_
  45.7 0.6 shard_map.72
  46.3 26.7 %all_to_all.10.back_ref = s16[64,2,2432]{2,1,0:T(2,128)(2,1)S(1)} all-to-all(s16[64,2,2432]{2,1,0:T(2,128)(2,1)S(1)} %shard_map.72), channel_id=1, replica_groups=mesh['store'=64,'batch'=4] {'store'}, dimensions={0} | all-to-all | bytes 1245184 | tf_op jit(solution)/shard_map/all_to_all | solution.py:336
  73.0 0.0 copy-done.3
  73.1 1.7 %shard_map.73 = (f32[128,1152]{1,0:T(8,128)}, f32[2,128]{1,0:T(2,128)}, f32[1,128]{1,0:T(1,128)}) custom-call(s32[1,128]{1,0:T(1,128)S(1)} %bitcast.5, s16[64,2,2432]{2,1,0:T(2,128)(2,1)S(1)} %all_to_all.10.back_ref), custom_call_target="tpu_custom_call" | custom-call | tf_op jit(solution)/shard_map/pallas_call | solution.py:338
Async XLA Ops:
  2.8 32.7 %all-to-all-start = ((bf16[64,2,2432]{2,1,0:T(2,128)(2,1)}), bf16[64,2,2432]{2,1,0:T(2,128)(2,1)S(1)}, u32[]{:S(2)}, u32[]{:S(2)}) async-start(bf16[64,2,2432]{2,1,0:T(2,128)(2,1)} %shard_map.67), calls=%async_computation | async-start | bytes 1245184 | tf_op jit(solution)/shard_map/all_to_all | solution.py:289
  17.1 2.3 %copy-start = (bf16[2048,1152]{1,0:T(8,128)(2,1)S(1)}, bf16[2048,1152]{1,0:T(8,128)(2,1)}, u32[]{:S(2)}) copy-start(bf16[2048,1152]{1,0:T(8,128)(2,1)} %store_hbm.1) | copy-start | bytes 14155780
  20.8 1.4 %copy-start.1 = (bf16[1024,1152]{1,0:T(8,128)(2,1)}, bf16[1024,1152]{1,0:T(8,128)(2,1)S(1)}, u32[]{:S(2)}) copy-start(bf16[1024,1152]{1,0:T(8,128)(2,1)S(1)} %get-tuple-element.22.rest_ref) | copy-start | bytes 7077892
  35.5 1.7 %copy-start.2 = (bf16[1024,1152]{1,0:T(8,128)(2,1)S(1)}, bf16[1024,1152]{1,0:T(8,128)(2,1)}, u32[]{:S(2)}) copy-start(bf16[1024,1152]{1,0:T(8,128)(2,1)} %copy-done.1) | copy-start | bytes 7077892
  39.0 6.7 %collective-permute-start.2 = (f32[1,128]{1,0:T(1,128)S(1)}, f32[1,128]{1,0:T(1,128)S(1)}, u32[]{:S(2)}, u32[]{:S(2)}) collective-permute-start(f32[1,128]{1,0:T(1,128)S(1)} %get-tuple-element.27.refs_0_), channel_id=1, source_target_pairs={{0,3},{1,0},{2,1},{3,2},{4,7},{5,4},{6,5},{7,6},{8,11},{9,8},{10,9... | collective-permute-start | bytes 1544 | tf_op jit(solution)/shard_map/ppermute | solution.py:239
  41.8 3.9 %collective-permute-start.1 = (f32[1,128]{1,0:T(1,128)S(1)}, f32[1,128]{1,0:T(1,128)S(1)}, u32[]{:S(2)}, u32[]{:S(2)}) collective-permute-start(f32[1,128]{1,0:T(1,128)S(1)} %get-tuple-element.27.refs_0_), channel_id=1, source_target_pairs={{0,1},{1,2},{2,3},{3,0},{4,5},{5,6},{6,7},{7,4},{8,9},{9,10},{10,1... | collective-permute-start | bytes 1544 | tf_op jit(solution)/shard_map/ppermute | solution.py:239
  41.8 3.9 %collective-permute-start = (f32[1,128]{1,0:T(1,128)S(1)}, f32[1,128]{1,0:T(1,128)S(1)}, u32[]{:S(2)}, u32[]{:S(2)}) collective-permute-start(f32[1,128]{1,0:T(1,128)S(1)} %get-tuple-element.27.refs_0_), channel_id=1, source_target_pairs={{0,2},{1,3},{2,0},{3,1},{4,6},{5,7},{6,4},{7,5},{8,10},{9,11},{10,... | collective-permute-start | bytes 1544 | tf_op jit(solution)/shard_map/ppermute | solution.py:239
  45.7 27.4 %copy-start.3 = (s32[128]{0:T(128)S(1)}, s32[128]{0:T(128)}, u32[]{:S(2)}) copy-start(s32[128]{0:T(128)} %param.5) | copy-start | bytes 1540

commit v6 on v5

--- a/solution.py
+++ b/solution.py
@@ -205,7 +205,7 @@
     return (high + low * (1.0 / LOW_UNIT)) * (1.0 / unit)
 
 
-def pick_kernel(cluster_ref, back_ref, near_ref, best_ref, novelty_ref):
+def pick_kernel(cluster_ref, back_ref, near_hbm, best_ref, novelty_ref, near_ref, sems):
     across, down, i, j = cluster_pairs(cluster_ref)
     clusters, pair, width = back_ref.shape
     features = (width - EXTRA) // SIDE
@@ -217,20 +217,30 @@
 
     pick = jnp.concatenate([pick, pick], axis=1)
 
-    def mine(halves):
+    def terms(halves):
         value = jnp.concatenate(halves, axis=0).astype(jnp.float32)
         high = jnp.floor(value * (1.0 / 256.0)) * 256.0
-        return dot(pick, jnp.concatenate([high, value - high], axis=0).astype(jnp.bfloat16), (1, 0))
+        return jnp.concatenate([high, value - high], axis=0).astype(jnp.bfloat16)
 
     extra = back_ref[:, :, SIDE * features :].reshape(step, EXTRA).astype(jnp.float32)
-    extra = mine([shifted(extra, h * (EXTRA // SIDE)) for h in range(SIDE)])
+    extra = dot(pick, terms([shifted(extra, h * (EXTRA // SIDE)) for h in range(SIDE)]), (1, 0))
     largest = jnp.exp(joined(extra[:, 4:5], extra[:, 5:6], LOG_UNIT))
-    rows = mine([back_ref[:, :, h * features : (h + 1) * features].reshape(step, features) for h in range(SIDE)])
-    near_ref[...] = rows * (largest * (1.0 / STEPS))
+    rows = terms([back_ref[:, :, h * features : (h + 1) * features].reshape(step, features) for h in range(SIDE)])
+    factor = largest * (1.0 / STEPS)
+    count = near_ref.shape[0] // sems.shape[0]
+    copies = []
+    for p in range(sems.shape[0]):
+        at = p * count
+        near_ref[at : at + count, :] = dot(pick[at : at + count], rows, (1, 0)) * factor[at : at + count]
+        span = pl.ds(at, count)
+        copies.append(pltpu.make_async_copy(near_ref.at[span], near_hbm.at[span], sems.at[p]))
+        copies[-1].start()
     extra = extra.T
     best_ref[0:1, :] = joined(extra[0:1], extra[1:2], COSINE_UNIT)
     best_ref[1:2, :] = joined(extra[2:3], extra[3:4], COSINE_UNIT)
     novelty_ref[...] = joined(extra[6:7], extra[7:8], NOVELTY_UNIT)
+    for copy in copies:
+        copy.wait()
 
 
 def over_batch(value):
@@ -342,6 +352,9 @@
             jax.ShapeDtypeStruct((2, rows_dev), jnp.float32),
             jax.ShapeDtypeStruct((1, rows_dev), jnp.float32),
         ),
+        in_specs=[vmem, vmem],
+        out_specs=(hbm, vmem, vmem),
+        scratch_shapes=[pltpu.VMEM((rows_dev, features), f32), pltpu.SemaphoreType.DMA((2,))],
         compiler_params=params,
     )(cluster_row, back)
     return (best.T, novelty[0], neighbours)

time: 75.1 us -> 75.7 us (level)
  no operation moved by 1% of the time
where the time goes in v6:
time: 75.7 us; the launch traced here: 75.4 us
  blocking collectives  26.7 us (35%)
  starting transfers between devices  17.5 us (23%)
  waiting for transfers between devices  12.6 us (17%)
  Pallas kernels  12.1 us (16%)
  local copies, waits for them, and re-layouts  5.13 us (7%)
    all_to_all x1, blocking collectives, body(): lax.all_to_all(back, 'store', split_axis=0, concat_axis=0, tiled=True)  26.7 us
    all_to_all x1, starting transfers between devices, body(): got = lax.all_to_all(send, 'store', split_axis=0, concat_axis=0, tiled=True)  13 us
    all_to_all x1, waiting for transfers between devices, body(): got = lax.all_to_all(send, 'store', split_axis=0, concat_axis=0, tiled=True)  12.6 us
    ppermute x3, starting transfers between devices, over_batch(): lax.ppermute(value, 'batch', [(i, (i + k) % n) for i in range(n)])  4.46 us
    unnamed x8, local copies, waits for them, and re-layouts  3.88 us
    pallas_call x1, Pallas kernels, body(): pl.pallas_call(pick_kernel, out_shape=(jax.ShapeDtypeStruct((rows_dev, fe...  2.35 us
    pallas_call x1, Pallas kernels, body(): pl.pallas_call(weigh_kernel, out_shape=(jax.ShapeDtypeStruct((slots, feat...  2.25 us
    pallas_call x1, Pallas kernels, body(): pl.pallas_call(place_kernel, out_shape=jax.ShapeDtypeStruct((clusters, pa...  2.16 us
  transfers between devices with their start and end apart: 4, of which 1 were waited for; matrix products, arithmetic and copies ran while one was open for 3% of the time, Pallas kernels for 5%

profile of v6, /device:TPU:1, one launch (start us, length us, event | category | flops | bytes accessed | tf_op | source)
XLA Modules:
  0.0 75.4 jit_solution(17859435268126159027)
XLA Ops:
  0.6 2.2 %shard_map.67 = bf16[64,2,2432]{2,1,0:T(2,128)(2,1)} custom-call(s32[1,128]{1,0:T(1,128)} %bitcast.4, bf16[128,1152]{1,0:T(8,128)(2,1)} %queries_hbm.1), custom_call_target="tpu_custom_call" | custom-call | tf_op jit(solution)/shard_map/pallas_call | solution.py:267
  2.8 13.0 %all-to-all-start = ((bf16[64,2,2432]{2,1,0:T(2,128)(2,1)}), bf16[64,2,2432]{2,1,0:T(2,128)(2,1)S(1)}, u32[]{:S(2)}, u32[]{:S(2)}) async-start(bf16[64,2,2432]{2,1,0:T(2,128)(2,1)} %shard_map.67), calls=%async_computation | async-start | bytes 1245184 | tf_op jit(solution)/shard_map/all_to_all | solution.py:299
  15.8 1.2 %dynamic_slice.3 = s32[1]{0:T(128)} dynamic-slice(s32[64]{0:T(128)} %param.7, s32[]{:T(128)S(6)} %select_n.3), dynamic_slice_sizes={1} | dynamic-slice | bytes 12 | tf_op jit(solution)/shard_map/dynamic_slice | solution.py:280
  17.1 0.0 copy-start
  17.1 2.3 %copy-done = bf16[2048,1152]{1,0:T(8,128)(2,1)S(1)} copy-done((bf16[2048,1152]{1,0:T(8,128)(2,1)S(1)}, bf16[2048,1152]{1,0:T(8,128)(2,1)}, u32[]{:S(2)}) %copy-start) | copy-done | bytes 4718616
  19.4 1.4 %shard_map.68 = (f32[1,2048]{1,0:T(1,128)S(1)}, bf16[1024,1152]{1,0:T(8,128)(2,1)S(1)}, bf16[1024,1152]{1,0:T(8,128)(2,1)S(1)}) custom-call(bf16[2048,1152]{1,0:T(8,128)(2,1)S(1)} %copy-done), custom_call_target="tpu_custom_call" | custom-call | flops 4718592 | bytes 4718592 | tf_op jit(solution)/shard_map/pallas_call | solution.py:286
  20.8 0.0 copy-start.1
  20.8 1.4 %copy-done.1 = bf16[1024,1152]{1,0:T(8,128)(2,1)} copy-done((bf16[1024,1152]{1,0:T(8,128)(2,1)}, bf16[1024,1152]{1,0:T(8,128)(2,1)S(1)}, u32[]{:S(2)}) %copy-start.1) | copy-done | bytes 2359320
  22.2 0.7 pad_add_fusion.info_ref
  22.9 12.6 %all-to-all-done.got_ref = bf16[64,2,2432]{2,1,0:T(2,128)(2,1)S(1)} async-done(((bf16[64,2,2432]{2,1,0:T(2,128)(2,1)}), bf16[64,2,2432]{2,1,0:T(2,128)(2,1)S(1)}, u32[]{:S(2)}, u32[]{:S(2)}) %all-to-all-start) | async-done | bytes 622624 | tf_op jit(solution)/shard_map/all_to_all | solution.py:299
  35.5 0.0 copy-start.2
  35.5 1.5 %shard_map.69 = (f32[256,1024]{1,0:T(8,128)S(1)}, bf16[256,1280]{1,0:T(8,128)(2,1)S(1)}, f32[3,256,128]{2,1,0:T(8,128)S(1)}) custom-call(s32[2]{0:T(128)S(1)} %pad_add_fusion.info_ref, bf16[64,2,2432]{2,1,0:T(2,128)(2,1)S(1)} %all-to-all-done.got_ref, bf16[1024,1152]{1,0:T(8,128)(2,1)S(1)} %get-tuple-element.17.near_ref, ...), custom_call_target="tpu_custom_call" | custom-call | flops 603979776 | bytes 2359296 | tf_op jit(solution)/shard_map/pallas_call | solution.py:302
  37.1 0.1 copy-done.2
  37.2 1.8 %shard_map.70 = (f32[256,1024]{1,0:T(8,128)S(1)}, f32[256,128]{1,0:T(8,128)S(1)}, f32[1,128]{1,0:T(1,128)S(1)}) custom-call(s32[2]{0:T(128)S(1)} %pad_add_fusion.info_ref, bf16[256,1280]{1,0:T(8,128)(2,1)S(1)} %get-tuple-element.20.rows_ref, f32[3,256,128]{2,1,0:T(8,128)S(1)} %get-tuple-element.21.state_ref, bf16[1024,1152]{1,0:T(8,128)(2,1)S(1)} %copy-done.2, ...), custom_call_target="tpu_custom_call" | custom-call | flops 603979776 | bytes 2359296 | tf_op jit(solution)/shard_map/pallas_call | solution.py:314
  39.0 2.8 %collective-permute-start.2 = (f32[1,128]{1,0:T(1,128)S(1)}, f32[1,128]{1,0:T(1,128)S(1)}, u32[]{:S(2)}, u32[]{:S(2)}) collective-permute-start(f32[1,128]{1,0:T(1,128)S(1)} %get-tuple-element.27.refs_0_), channel_id=1, source_target_pairs={{0,3},{1,0},{2,1},{3,2},{4,7},{5,4},{6,5},{7,6},{8,11},{9,8},{10,9... | collective-permute-start | bytes 1544 | tf_op jit(solution)/shard_map/ppermute | solution.py:249
  41.8 0.0 collective-permute-start.1
  41.8 1.6 %collective-permute-start = (f32[1,128]{1,0:T(1,128)S(1)}, f32[1,128]{1,0:T(1,128)S(1)}, u32[]{:S(2)}, u32[]{:S(2)}) collective-permute-start(f32[1,128]{1,0:T(1,128)S(1)} %get-tuple-element.27.refs_0_), channel_id=1, source_target_pairs={{0,2},{1,3},{2,0},{3,1},{4,6},{5,7},{6,4},{7,5},{8,10},{9,11},{10,... | collective-permute-start | bytes 1544 | tf_op jit(solution)/shard_map/ppermute | solution.py:249
  43.4 2.2 %shard_map.71 = (f32[256,1152]{1,0:T(8,128)S(1)}, f32[256,128]{1,0:T(8,128)S(1)}) custom-call(s32[2]{0:T(128)S(1)} %pad_add_fusion.info_ref, f32[256,1024]{1,0:T(8,128)S(1)} %get-tuple-element.19.cos_near_ref, f32[256,1024]{1,0:T(8,128)S(1)} %get-tuple-element.23.cos_rest_ref, f32[256,128]{1,0:T(8,128)S(1)} %get-tuple-element.24.best_ref, ...), custom_call_target="tpu_custom_call" | custom-call | flops 2415919104 | bytes 18874368 | tf_op jit(solution)/shard_map/pallas_call | solution.py:327
  45.7 0.0 copy-start.3
  45.7 0.0 collective-permute-done.2.refs_3_
  45.7 0.0 collective-permute-done.1.refs_2_
  45.7 0.0 collective-permute-done.refs_1_
  45.7 0.6 shard_map.72
  46.3 26.7 %all_to_all.10.back_ref = s16[64,2,2432]{2,1,0:T(2,128)(2,1)S(1)} all-to-all(s16[64,2,2432]{2,1,0:T(2,128)(2,1)S(1)} %shard_map.72), channel_id=1, replica_groups=mesh['store'=64,'batch'=4] {'store'}, dimensions={0} | all-to-all | bytes 1245184 | tf_op jit(solution)/shard_map/all_to_all | solution.py:346
  73.0 0.0 copy-done.3
  73.1 2.3 %shard_map.73 = (f32[128,1152]{1,0:T(8,128)}, f32[2,128]{1,0:T(2,128)}, f32[1,128]{1,0:T(1,128)}) custom-call(s32[1,128]{1,0:T(1,128)S(1)} %bitcast.5, s16[64,2,2432]{2,1,0:T(2,128)(2,1)S(1)} %all_to_all.10.back_ref), custom_call_target="tpu_custom_call" | custom-call | tf_op jit(solution)/shard_map/pallas_call | solution.py:348
Async XLA Ops:
  2.8 32.7 %all-to-all-start = ((bf16[64,2,2432]{2,1,0:T(2,128)(2,1)}), bf16[64,2,2432]{2,1,0:T(2,128)(2,1)S(1)}, u32[]{:S(2)}, u32[]{:S(2)}) async-start(bf16[64,2,2432]{2,1,0:T(2,128)(2,1)} %shard_map.67), calls=%async_computation | async-start | bytes 1245184 | tf_op jit(solution)/shard_map/all_to_all | solution.py:299
  17.1 2.3 %copy-start = (bf16[2048,1152]{1,0:T(8,128)(2,1)S(1)}, bf16[2048,1152]{1,0:T(8,128)(2,1)}, u32[]{:S(2)}) copy-start(bf16[2048,1152]{1,0:T(8,128)(2,1)} %store_hbm.1) | copy-start | bytes 14155780
  20.8 1.4 %copy-start.1 = (bf16[1024,1152]{1,0:T(8,128)(2,1)}, bf16[1024,1152]{1,0:T(8,128)(2,1)S(1)}, u32[]{:S(2)}) copy-start(bf16[1024,1152]{1,0:T(8,128)(2,1)S(1)} %get-tuple-element.22.rest_ref) | copy-start | bytes 7077892
  35.5 1.7 %copy-start.2 = (bf16[1024,1152]{1,0:T(8,128)(2,1)S(1)}, bf16[1024,1152]{1,0:T(8,128)(2,1)}, u32[]{:S(2)}) copy-start(bf16[1024,1152]{1,0:T(8,128)(2,1)} %copy-done.1) | copy-start | bytes 7077892
  39.0 6.7 %collective-permute-start.2 = (f32[1,128]{1,0:T(1,128)S(1)}, f32[1,128]{1,0:T(1,128)S(1)}, u32[]{:S(2)}, u32[]{:S(2)}) collective-permute-start(f32[1,128]{1,0:T(1,128)S(1)} %get-tuple-element.27.refs_0_), channel_id=1, source_target_pairs={{0,3},{1,0},{2,1},{3,2},{4,7},{5,4},{6,5},{7,6},{8,11},{9,8},{10,9... | collective-permute-start | bytes 1544 | tf_op jit(solution)/shard_map/ppermute | solution.py:249
  41.8 3.9 %collective-permute-start.1 = (f32[1,128]{1,0:T(1,128)S(1)}, f32[1,128]{1,0:T(1,128)S(1)}, u32[]{:S(2)}, u32[]{:S(2)}) collective-permute-start(f32[1,128]{1,0:T(1,128)S(1)} %get-tuple-element.27.refs_0_), channel_id=1, source_target_pairs={{0,1},{1,2},{2,3},{3,0},{4,5},{5,6},{6,7},{7,4},{8,9},{9,10},{10,1... | collective-permute-start | bytes 1544 | tf_op jit(solution)/shard_map/ppermute | solution.py:249
  41.8 3.9 %collective-permute-start = (f32[1,128]{1,0:T(1,128)S(1)}, f32[1,128]{1,0:T(1,128)S(1)}, u32[]{:S(2)}, u32[]{:S(2)}) collective-permute-start(f32[1,128]{1,0:T(1,128)S(1)} %get-tuple-element.27.refs_0_), channel_id=1, source_target_pairs={{0,2},{1,3},{2,0},{3,1},{4,6},{5,7},{6,4},{7,5},{8,10},{9,11},{10,... | collective-permute-start | bytes 1544 | tf_op jit(solution)/shard_map/ppermute | solution.py:249
  45.7 27.4 %copy-start.3 = (s32[128]{0:T(128)S(1)}, s32[128]{0:T(128)}, u32[]{:S(2)}) copy-start(s32[128]{0:T(128)} %param.5) | copy-start | bytes 1540

commit v7 on v5

--- a/solution.py
+++ b/solution.py
@@ -13,6 +13,7 @@
 EXTRA = 128
 SIDE = 2
 STEPS = 32767.0
+NOT_LIVE = -1e30
 COSINE_UNIT = 16384.0
 NOVELTY_UNIT = 8192.0
 LOG_UNIT = 256.0
@@ -92,14 +93,14 @@
     return [high, jnp.round((value * unit - high) * LOW_UNIT)]
 
 
-def cosines(rows, row_scale, held_ref, scale_ref, live, base, one, two, cos_ref):
+def cosines(rows, held_ref, scale_ref, live, base, one, two, cos_ref):
     lane = lax.broadcasted_iota(jnp.int32, one.shape, 1)
     for t in range(0, held_ref.shape[0], TILE):
         raw = dot(rows, held_ref[t : t + TILE, :], (1, 1))
         for h in range(0, TILE, 128):
             at = t + h
-            cosine = raw[:, h : h + 128] * row_scale * scale_ref[:, base + at : base + at + 128]
-            cosine = jnp.where(lane < live - base - at, cosine, -2.0)
+            cosine = raw[:, h : h + 128] * scale_ref[:, base + at : base + at + 128]
+            cosine = jnp.where(lane < live - base - at, cosine, NOT_LIVE)
             cos_ref[:, at : at + 128] = cosine
             two = jnp.maximum(two, jnp.minimum(one, cosine))
             one = jnp.maximum(one, cosine)
@@ -116,12 +117,10 @@
         span = slice(h * step, (h + 1) * step)
         rows_ref[span, :features] = got_ref[:, :, h * features : (h + 1) * features].reshape(step, features)
         rows_ref[span, features:] = shifted(extra, h * (EXTRA // SIDE)).astype(rows_ref.dtype)
-    rows = rows_ref[:, :features]
-    wide = rows.astype(jnp.float32)
-    row_scale = lax.rsqrt(jnp.sum(wide * wide, axis=1, keepdims=True) + epsilon)
-    state_ref[0] = jnp.broadcast_to(row_scale, (slots, 128))
-    one = jnp.full((slots, 128), -3.0, jnp.float32)
-    state_ref[1], state_ref[2] = cosines(rows, row_scale, near_ref, scale_ref, info_ref[0], 0, one, one, cos_ref)
+    one = jnp.full((slots, 128), 2.0 * NOT_LIVE, jnp.float32)
+    state_ref[0], state_ref[1] = cosines(
+        rows_ref[:, :features], near_ref, scale_ref, info_ref[0], 0, one, one, cos_ref
+    )
 
 
 def rest_kernel(
@@ -135,14 +134,18 @@
     index = (slot % (2 * n_store) // 2 * n_batch + batch) * rows_dev + tail[:, :1].astype(jnp.int32)
     recency = jnp.exp(index.astype(jnp.float32) * growth) * tail[:, 1:2]
     base = scale_ref.shape[1] - rest_ref.shape[0]
-    one, two = cosines(
-        rows_ref[:, :features], state_ref[0][:, :1], rest_ref, scale_ref, live, base, state_ref[1], state_ref[2], cos_ref
-    )
+    rows = rows_ref[:, :features]
+    one, two = cosines(rows, rest_ref, scale_ref, live, base, state_ref[0], state_ref[1], cos_ref)
+    wide = rows.astype(jnp.float32)
+    row_scale = lax.rsqrt(jnp.sum(wide * wide, axis=1, keepdims=True) + epsilon)
     lane = lax.broadcasted_iota(jnp.int32, (slots, 128), 1)
     first = jnp.max(one, axis=1, keepdims=True)
     holder = jnp.min(jnp.where(one == first, lane, 128), axis=1, keepdims=True)
     second = jnp.max(jnp.where(lane == holder, two, one), axis=1, keepdims=True)
-    best_ref[...] = jnp.where(lane == 0, first, second)
+    best_ref[...] = jnp.where(
+        lane == 0, first * row_scale, jnp.where(lane == 1, second * row_scale, jnp.where(lane == 2, first, row_scale))
+    )
+    first = first * row_scale
     across = lax.broadcasted_iota(jnp.int32, sums_ref.shape, 1)
     sums_ref[...] = jnp.where(
         across == 0,
@@ -154,12 +157,13 @@
 def weigh_kernel(info_ref, cos_near_ref, cos_rest_ref, best_ref, near_ref, rest_ref, weighted_ref, total_ref, expo_ref):
     slots, near = cos_near_ref.shape
     live = info_ref[0]
-    first = best_ref[:, :1]
+    first = best_ref[:, 2:3]
+    factor = normalized_sharpness * best_ref[:, 3:4]
     lane = lax.broadcasted_iota(jnp.int32, (slots, 128), 1)
     total = jnp.zeros((slots, 128), jnp.float32)
     for cos_ref, base in ((cos_near_ref, 0), (cos_rest_ref, near)):
         for at in range(0, cos_ref.shape[1], 128):
-            expo = jnp.exp(normalized_sharpness * (cos_ref[:, at : at + 128] - first))
+            expo = jnp.exp(factor * (cos_ref[:, at : at + 128] - first))
             expo = jnp.where(lane < live - base - at, expo, 0.0)
             total = total + expo
             expo_ref[:, base + at : base + at + 128] = expo.astype(jnp.bfloat16)
@@ -294,7 +298,7 @@
         out_shape=(
             jax.ShapeDtypeStruct((slots, near), f32),
             jax.ShapeDtypeStruct((slots, width), bf16),
-            jax.ShapeDtypeStruct((3, slots, 128), f32),
+            jax.ShapeDtypeStruct((2, slots, 128), f32),
         ),
         in_specs=[smem, vmem, vmem, vmem],
         out_specs=(vmem,) * 3,

time: 75.1 us -> 75.1 us (level)
  no operation moved by 1% of the time
where the time goes in v7:
time: 75.1 us; the launch traced here: 74.8 us
  blocking collectives  26.6 us (35%)
  starting transfers between devices  17.4 us (23%)
  waiting for transfers between devices  12.6 us (17%)
  Pallas kernels  11.5 us (15%)
  local copies, waits for them, and re-layouts  5.17 us (7%)
    all_to_all x1, blocking collectives, body(): lax.all_to_all(back, 'store', split_axis=0, concat_axis=0, tiled=True)  26.6 us
    all_to_all x1, starting transfers between devices, body(): got = lax.all_to_all(send, 'store', split_axis=0, concat_axis=0, tiled=True)  13 us
    all_to_all x1, waiting for transfers between devices, body(): got = lax.all_to_all(send, 'store', split_axis=0, concat_axis=0, tiled=True)  12.6 us
    ppermute x3, starting transfers between devices, over_batch(): lax.ppermute(value, 'batch', [(i, (i + k) % n) for i in range(n)])  4.45 us
    unnamed x8, local copies, waits for them, and re-layouts  3.93 us
    pallas_call x1, Pallas kernels, body(): pl.pallas_call(weigh_kernel, out_shape=(jax.ShapeDtypeStruct((slots, feat...  2.32 us
    pallas_call x1, Pallas kernels, body(): pl.pallas_call(place_kernel, out_shape=jax.ShapeDtypeStruct((clusters, pa...  2.16 us
    pallas_call x1, Pallas kernels, body(): pl.pallas_call(functools.partial(rest_kernel, growth, n_batch, rows_dev,...  1.84 us
  transfers between devices with their start and end apart: 4, of which 1 were waited for; matrix products, arithmetic and copies ran while one was open for 3% of the time, Pallas kernels for 5%

profile of v7, /device:TPU:1, one launch (start us, length us, event | category | flops | bytes accessed | tf_op | source)
XLA Modules:
  0.0 74.8 jit_solution(13774375093673562251)
XLA Ops:
  0.6 2.2 %shard_map.67 = bf16[64,2,2432]{2,1,0:T(2,128)(2,1)} custom-call(s32[1,128]{1,0:T(1,128)} %bitcast.4, bf16[128,1152]{1,0:T(8,128)(2,1)} %queries_hbm.1), custom_call_target="tpu_custom_call" | custom-call | tf_op jit(solution)/shard_map/pallas_call | solution.py:261
  2.8 13.0 %all-to-all-start = ((bf16[64,2,2432]{2,1,0:T(2,128)(2,1)}), bf16[64,2,2432]{2,1,0:T(2,128)(2,1)S(1)}, u32[]{:S(2)}, u32[]{:S(2)}) async-start(bf16[64,2,2432]{2,1,0:T(2,128)(2,1)} %shard_map.67), calls=%async_computation | async-start | bytes 1245184 | tf_op jit(solution)/shard_map/all_to_all | solution.py:293
  15.8 1.2 %dynamic_slice.3 = s32[1]{0:T(128)} dynamic-slice(s32[64]{0:T(128)} %param.7, s32[]{:T(128)S(6)} %select_n.3), dynamic_slice_sizes={1} | dynamic-slice | bytes 12 | tf_op jit(solution)/shard_map/dynamic_slice | solution.py:274
  17.1 0.0 copy-start
  17.1 2.3 %copy-done = bf16[2048,1152]{1,0:T(8,128)(2,1)S(1)} copy-done((bf16[2048,1152]{1,0:T(8,128)(2,1)S(1)}, bf16[2048,1152]{1,0:T(8,128)(2,1)}, u32[]{:S(2)}) %copy-start) | copy-done | bytes 4718616
  19.4 1.4 %shard_map.68 = (f32[1,2048]{1,0:T(1,128)S(1)}, bf16[1024,1152]{1,0:T(8,128)(2,1)S(1)}, bf16[1024,1152]{1,0:T(8,128)(2,1)S(1)}) custom-call(bf16[2048,1152]{1,0:T(8,128)(2,1)S(1)} %copy-done), custom_call_target="tpu_custom_call" | custom-call | flops 4718592 | bytes 4718592 | tf_op jit(solution)/shard_map/pallas_call | solution.py:280
  20.8 0.0 copy-start.1
  20.8 1.4 %copy-done.1 = bf16[1024,1152]{1,0:T(8,128)(2,1)} copy-done((bf16[1024,1152]{1,0:T(8,128)(2,1)}, bf16[1024,1152]{1,0:T(8,128)(2,1)S(1)}, u32[]{:S(2)}) %copy-start.1) | copy-done | bytes 2359320
  22.2 0.7 pad_add_fusion.info_ref
  22.9 12.6 %all-to-all-done.got_ref = bf16[64,2,2432]{2,1,0:T(2,128)(2,1)S(1)} async-done(((bf16[64,2,2432]{2,1,0:T(2,128)(2,1)}), bf16[64,2,2432]{2,1,0:T(2,128)(2,1)S(1)}, u32[]{:S(2)}, u32[]{:S(2)}) %all-to-all-start) | async-done | bytes 622624 | tf_op jit(solution)/shard_map/all_to_all | solution.py:293
  35.5 0.0 copy-start.2
  35.5 1.5 %shard_map.69 = (f32[256,1024]{1,0:T(8,128)S(1)}, bf16[256,1280]{1,0:T(8,128)(2,1)S(1)}, f32[2,256,128]{2,1,0:T(8,128)S(1)}) custom-call(s32[2]{0:T(128)S(1)} %pad_add_fusion.info_ref, bf16[64,2,2432]{2,1,0:T(2,128)(2,1)S(1)} %all-to-all-done.got_ref, bf16[1024,1152]{1,0:T(8,128)(2,1)S(1)} %get-tuple-element.17.near_ref, ...), custom_call_target="tpu_custom_call" | custom-call | flops 603979776 | bytes 2359296 | tf_op jit(solution)/shard_map/pallas_call | solution.py:296
  37.0 0.2 copy-done.2
  37.2 1.8 %shard_map.70 = (f32[256,1024]{1,0:T(8,128)S(1)}, f32[256,128]{1,0:T(8,128)S(1)}, f32[1,128]{1,0:T(1,128)S(1)}) custom-call(s32[2]{0:T(128)S(1)} %pad_add_fusion.info_ref, bf16[256,1280]{1,0:T(8,128)(2,1)S(1)} %get-tuple-element.20.rows_ref, f32[2,256,128]{2,1,0:T(8,128)S(1)} %get-tuple-element.21.state_ref, bf16[1024,1152]{1,0:T(8,128)(2,1)S(1)} %copy-done.2, ...), custom_call_target="tpu_custom_call" | custom-call | flops 603979776 | bytes 2359296 | tf_op jit(solution)/shard_map/pallas_call | solution.py:308
  39.0 2.8 %collective-permute-start.2 = (f32[1,128]{1,0:T(1,128)S(1)}, f32[1,128]{1,0:T(1,128)S(1)}, u32[]{:S(2)}, u32[]{:S(2)}) collective-permute-start(f32[1,128]{1,0:T(1,128)S(1)} %get-tuple-element.27.refs_0_), channel_id=1, source_target_pairs={{0,3},{1,0},{2,1},{3,2},{4,7},{5,4},{6,5},{7,6},{8,11},{9,8},{10,9... | collective-permute-start | bytes 1544 | tf_op jit(solution)/shard_map/ppermute | solution.py:243
  41.8 0.0 collective-permute-start.1
  41.8 1.6 %collective-permute-start = (f32[1,128]{1,0:T(1,128)S(1)}, f32[1,128]{1,0:T(1,128)S(1)}, u32[]{:S(2)}, u32[]{:S(2)}) collective-permute-start(f32[1,128]{1,0:T(1,128)S(1)} %get-tuple-element.27.refs_0_), channel_id=1, source_target_pairs={{0,2},{1,3},{2,0},{3,1},{4,6},{5,7},{6,4},{7,5},{8,10},{9,11},{10,... | collective-permute-start | bytes 1544 | tf_op jit(solution)/shard_map/ppermute | solution.py:243
  43.5 2.3 %shard_map.71 = (f32[256,1152]{1,0:T(8,128)S(1)}, f32[256,128]{1,0:T(8,128)S(1)}) custom-call(s32[2]{0:T(128)S(1)} %pad_add_fusion.info_ref, f32[256,1024]{1,0:T(8,128)S(1)} %get-tuple-element.19.cos_near_ref, f32[256,1024]{1,0:T(8,128)S(1)} %get-tuple-element.23.cos_rest_ref, f32[256,128]{1,0:T(8,128)S(1)} %get-tuple-element.24.best_ref, ...), custom_call_target="tpu_custom_call" | custom-call | flops 2415919104 | bytes 18874368 | tf_op jit(solution)/shard_map/pallas_call | solution.py:321
  45.8 0.0 copy-start.3
  45.8 0.0 collective-permute-done.2.refs_3_
  45.8 0.0 collective-permute-done.1.refs_2_
  45.8 0.0 collective-permute-done.refs_1_
  45.8 0.6 shard_map.72
  46.5 26.6 %all_to_all.10.back_ref = s16[64,2,2432]{2,1,0:T(2,128)(2,1)S(1)} all-to-all(s16[64,2,2432]{2,1,0:T(2,128)(2,1)S(1)} %shard_map.72), channel_id=1, replica_groups=mesh['store'=64,'batch'=4] {'store'}, dimensions={0} | all-to-all | bytes 1245184 | tf_op jit(solution)/shard_map/all_to_all | solution.py:340
  73.1 0.0 copy-done.3
  73.1 1.7 %shard_map.73 = (f32[128,1152]{1,0:T(8,128)}, f32[2,128]{1,0:T(2,128)}, f32[1,128]{1,0:T(1,128)}) custom-call(s32[1,128]{1,0:T(1,128)S(1)} %bitcast.5, s16[64,2,2432]{2,1,0:T(2,128)(2,1)S(1)} %all_to_all.10.back_ref), custom_call_target="tpu_custom_call" | custom-call | tf_op jit(solution)/shard_map/pallas_call | solution.py:342
Async XLA Ops:
  2.8 32.7 %all-to-all-start = ((bf16[64,2,2432]{2,1,0:T(2,128)(2,1)}), bf16[64,2,2432]{2,1,0:T(2,128)(2,1)S(1)}, u32[]{:S(2)}, u32[]{:S(2)}) async-start(bf16[64,2,2432]{2,1,0:T(2,128)(2,1)} %shard_map.67), calls=%async_computation | async-start | bytes 1245184 | tf_op jit(solution)/shard_map/all_to_all | solution.py:293
  17.1 2.3 %copy-start = (bf16[2048,1152]{1,0:T(8,128)(2,1)S(1)}, bf16[2048,1152]{1,0:T(8,128)(2,1)}, u32[]{:S(2)}) copy-start(bf16[2048,1152]{1,0:T(8,128)(2,1)} %store_hbm.1) | copy-start | bytes 14155780
  20.8 1.4 %copy-start.1 = (bf16[1024,1152]{1,0:T(8,128)(2,1)}, bf16[1024,1152]{1,0:T(8,128)(2,1)S(1)}, u32[]{:S(2)}) copy-start(bf16[1024,1152]{1,0:T(8,128)(2,1)S(1)} %get-tuple-element.22.rest_ref) | copy-start | bytes 7077892
  35.5 1.7 %copy-start.2 = (bf16[1024,1152]{1,0:T(8,128)(2,1)S(1)}, bf16[1024,1152]{1,0:T(8,128)(2,1)}, u32[]{:S(2)}) copy-start(bf16[1024,1152]{1,0:T(8,128)(2,1)} %copy-done.1) | copy-start | bytes 7077892
  39.0 6.8 %collective-permute-start.2 = (f32[1,128]{1,0:T(1,128)S(1)}, f32[1,128]{1,0:T(1,128)S(1)}, u32[]{:S(2)}, u32[]{:S(2)}) collective-permute-start(f32[1,128]{1,0:T(1,128)S(1)} %get-tuple-element.27.refs_0_), channel_id=1, source_target_pairs={{0,3},{1,0},{2,1},{3,2},{4,7},{5,4},{6,5},{7,6},{8,11},{9,8},{10,9... | collective-permute-start | bytes 1544 | tf_op jit(solution)/shard_map/ppermute | solution.py:243
  41.8 4.0 %collective-permute-start.1 = (f32[1,128]{1,0:T(1,128)S(1)}, f32[1,128]{1,0:T(1,128)S(1)}, u32[]{:S(2)}, u32[]{:S(2)}) collective-permute-start(f32[1,128]{1,0:T(1,128)S(1)} %get-tuple-element.27.refs_0_), channel_id=1, source_target_pairs={{0,1},{1,2},{2,3},{3,0},{4,5},{5,6},{6,7},{7,4},{8,9},{9,10},{10,1... | collective-permute-start | bytes 1544 | tf_op jit(solution)/shard_map/ppermute | solution.py:243
  41.8 4.0 %collective-permute-start = (f32[1,128]{1,0:T(1,128)S(1)}, f32[1,128]{1,0:T(1,128)S(1)}, u32[]{:S(2)}, u32[]{:S(2)}) collective-permute-start(f32[1,128]{1,0:T(1,128)S(1)} %get-tuple-element.27.refs_0_), channel_id=1, source_target_pairs={{0,2},{1,3},{2,0},{3,1},{4,6},{5,7},{6,4},{7,5},{8,10},{9,11},{10,... | collective-permute-start | bytes 1544 | tf_op jit(solution)/shard_map/ppermute | solution.py:243
  45.8 27.3 %copy-start.3 = (s32[128]{0:T(128)S(1)}, s32[128]{0:T(128)}, u32[]{:S(2)}) copy-start(s32[128]{0:T(128)} %param.5) | copy-start | bytes 1540
